TPU v7x, 256 devices: a whole 4x4x8 slice. The times are simulated.
256 devices in a mesh: seq: 32 (over x_lo, z, core), band: 8 (over y, x_hi).
Axes of the slice: x: 4 (x_hi: 2, x_lo: 2; x = x_hi * 2 + x_lo), y: 4, z: 8, core: 2. Of those that a mesh axis runs over, the one named last changes fastest.
Arguments:
- tokens: bfloat16 [4096, 1024], P('seq', 'band'), may hold values from -6 to 6
- mappable: int32 [4096], P('seq'), may hold values 0 or 1
- attn_gain: float32 [1024], replicated, may hold values from 0.1 to 1.9
- w_query: bfloat16 [1024, 1024], P(None, 'band'), may hold values from -1 to 1
- w_key: bfloat16 [1024, 1024], P(None, 'band'), may hold values from -4 to 4
- w_value: bfloat16 [1024, 1024], P(None, 'band'), may hold values from -0.1875 to 0.1875
- w_out: bfloat16 [1024, 1024], P('band'), may hold values from -0.75 to 0.75
- w_left: bfloat16 [1024, 128], replicated, may hold values from -0.1875 to 0.1875
- w_right: bfloat16 [1024, 128], replicated, may hold values from -0.1875 to 0.1875
- conv_gain: float32 [2, 128], replicated, may hold values from 0.1 to 1.9
- conv_kernel: bfloat16 [2, 3, 3, 128, 128], replicated, may hold values from -0.1875 to 0.1875
- conv_bias: float32 [2, 128], replicated, may hold values from -3 to 3
- contact_weight: float32 [128], replicated, may hold values from -0.5 to 0.5
Outputs:
- trunk_out: bfloat16 [4096, 1024], P('seq', 'band')
- contacts: float32 [4096, 256], P('seq', 'band')
All inputs are finite; a program needn't handle non-finite values. No bound on the sum of `mappable` on one device may be relied on, other than what follows from the above.
Results may differ from a plain program's by a relative error of at most 0.035.
Values may be sent and summed in bfloat16 or wider, within the bound.
A program may use at most 64 MiB of HBM per device.

v0:
```python
import jax
import jax.numpy as jnp
from jax import lax
from jax.sharding import PartitionSpec as P

HEAD = 128
CONVS = 2
DIAG = 32


epsilon = 1e-06


def passed_along(value, axis, steps):
    count = lax.axis_size(axis)
    initial, last = (max(0, -steps), min(count, count - steps))
    return lax.ppermute(value, axis, [(source, source + steps) for source in range(initial, last)])


def extended(x, sides, width):
    for axis, dim in sides:
        size, length = (lax.axis_size(axis), x.shape[dim])
        up = [(i, (i + 1) % size) for i in range(size - 1)]
        down = [(j, i) for i, j in up]
        last = lax.slice_in_dim(x, length - width, length, axis=dim)
        initial = lax.slice_in_dim(x, 0, width, axis=dim)
        before = lax.ppermute(last, axis, up)
        after = lax.ppermute(initial, axis, down)
        x = jnp.concatenate([before, x, after], axis=dim)
    return x


def rms_scale(values, gain):
    floats = values.astype(jnp.float32)
    return floats * lax.rsqrt(jnp.mean(floats * floats, axis=-1, keepdims=True) + epsilon) * gain


def shear_conv(padded, kernel, spread):
    out_rows = padded.shape[0] - 2 * spread
    out_diags = padded.shape[1] - 4 * spread
    windows = []
    for tap_row in range(3):
        for tap_col in range(3):
            row_first = spread * tap_row
            diag_first = 2 * spread + spread * (tap_col - tap_row)
            windows.append(
                padded[row_first : row_first + out_rows, diag_first : diag_first + out_diags]
            )
    stacked = jnp.concatenate(windows, axis=-1)
    flat_kernel = kernel.reshape(9 * kernel.shape[-2], kernel.shape[-1])
    return jnp.einsum("aek,kf->aef", stacked, flat_kernel, preferred_element_type=jnp.float32)


def valid_cells(row_first, diag_first, row_count, diag_count, length, band_width):
    rows_glob = row_first + jnp.arange(row_count, dtype=jnp.int32)
    diags_glob = diag_first + jnp.arange(diag_count, dtype=jnp.int32)
    inside = (
        (rows_glob[:, None] >= 0)
        & (rows_glob[:, None] < length)
        & (diags_glob[None, :] >= 0)
        & (diags_glob[None, :] < band_width)
        & (rows_glob[:, None] + diags_glob[None, :] < length)
    )
    return jnp.where(inside, 1.0, 0.0).astype(jnp.float32)[:, :, None]


def local(
    tokens,
    mappable,
    attn_gain,
    w_query,
    w_key,
    w_value,
    w_out,
    w_left,
    w_right,
    conv_gain,
    conv_kernel,
    conv_bias,
    contact_weight,
):
    row_count = tokens.shape[0]
    feature_share = tokens.shape[1]
    heads_here = w_query.shape[1] // HEAD
    seq_index = lax.axis_index("seq")
    band_index = lax.axis_index("band")
    length = row_count * lax.axis_size("seq")
    band_width = DIAG * lax.axis_size("band")
    gathered = lax.all_gather(tokens, "band", axis=1, tiled=True)
    normed = rms_scale(gathered, attn_gain).astype(jnp.bfloat16)
    query = jnp.dot(normed, w_query, preferred_element_type=jnp.float32).astype(jnp.bfloat16)
    key_rows = jnp.dot(normed, w_key, preferred_element_type=jnp.float32).astype(jnp.bfloat16)
    value = jnp.dot(normed, w_value, preferred_element_type=jnp.float32).astype(jnp.bfloat16)
    key_offset = ((mappable - 1).astype(jnp.float32) * 1000000000.0).astype(jnp.bfloat16)
    query_heads = query.reshape(row_count, heads_here, HEAD)
    row_top = jnp.full((heads_here, row_count), -jnp.inf, jnp.float32)
    weight_sum = jnp.zeros((heads_here, row_count), jnp.float32)
    mixed_sum = jnp.zeros((heads_here, row_count, HEAD), jnp.float32)
    key_piece = lax.all_gather(key_rows, "seq", axis=0, tiled=True)
    value_piece = lax.all_gather(value, "seq", axis=0, tiled=True)
    offset_piece = lax.all_gather(key_offset, "seq", axis=0, tiled=True)
    piece_rows = key_piece.shape[0]
    key_heads = key_piece.reshape(piece_rows, heads_here, HEAD)
    value_heads = value_piece.reshape(piece_rows, heads_here, HEAD)
    scores = (
        jnp.einsum("thd,nhd->htn", query_heads, key_heads, preferred_element_type=jnp.float32)
        * HEAD ** (-0.5)
        + offset_piece.astype(jnp.float32)[None, None, :]
    )
    new_top = jnp.max(scores, axis=2)
    weights = jnp.exp(scores - new_top[:, :, None])
    fade = jnp.exp(row_top - new_top)
    weight_sum = weight_sum * fade + jnp.sum(weights, axis=2)
    mixed_sum = mixed_sum * fade[:, :, None] + jnp.einsum(
        "htn,nhd->htd",
        weights.astype(jnp.bfloat16),
        value_heads,
        preferred_element_type=jnp.float32,
    )
    row_top, weight_sum, mixed_sum = (new_top, weight_sum, mixed_sum)
    attended = (
        (mixed_sum / weight_sum[:, :, None])
        .astype(jnp.bfloat16)
        .transpose(1, 0, 2)
        .reshape(row_count, heads_here * HEAD)
    )
    projected = jnp.dot(attended, w_out, preferred_element_type=jnp.float32)
    keep_rows = mappable.astype(jnp.bfloat16)[:, None]
    summed = lax.psum_scatter(
        projected.astype(jnp.bfloat16), "band", scatter_dimension=1, tiled=True
    ).astype(jnp.float32)
    trunk_out = (tokens.astype(jnp.float32) + summed).astype(jnp.bfloat16)
    rows_left = lax.dynamic_slice_in_dim(w_left, band_index * feature_share, feature_share, 0)
    rows_right = lax.dynamic_slice_in_dim(w_right, band_index * feature_share, feature_share, 0)
    part_left, part_right = (
        lax.psum(
            jnp.dot(trunk_out, rows_left, preferred_element_type=jnp.float32).astype(jnp.bfloat16),
            "band",
        ).astype(jnp.float32),
        lax.psum(
            jnp.dot(trunk_out, rows_right, preferred_element_type=jnp.float32).astype(jnp.bfloat16),
            "band",
        ).astype(jnp.float32),
    )
    left_side = part_left.astype(jnp.bfloat16) * keep_rows
    right_side = part_right.astype(jnp.bfloat16) * keep_rows
    row_start = seq_index * row_count
    diag_start = band_index * DIAG
    span_rows = row_count + DIAG
    following = passed_along(right_side, "seq", -1)
    window = jnp.concatenate([right_side, following], axis=0)
    block_reach = band_index * DIAG // row_count
    most_reach = (lax.axis_size("band") - 1) * DIAG // row_count

    def advance(turn_index, carry):
        current, chosen = carry
        current = passed_along(current, "seq", -1)
        chosen = jnp.where(block_reach == turn_index + 1, current, chosen)
        return (current, chosen)

    window = lax.fori_loop(0, most_reach, advance, (window, window))[1]
    first_row = band_index * DIAG % row_count
    window_rows = lax.dynamic_slice_in_dim(window, first_row, span_rows, 0)
    repeated = jnp.tile(window_rows, (row_count + 1, 1))[: row_count * (span_rows + 1)]
    hankel_rows = repeated.reshape(row_count, span_rows + 1, window_rows.shape[1])[:, :DIAG]
    pair_field = (
        left_side[:, None, :].astype(jnp.float32)
        * hankel_rows.astype(jnp.float32)
        * valid_cells(row_start, diag_start, row_count, DIAG, length, band_width)
    ).astype(jnp.bfloat16)
    tile_valid = valid_cells(row_start, diag_start, row_count, DIAG, length, band_width)
    for layer_index in range(CONVS):
        spread = 2**layer_index
        activated = jax.nn.gelu(rms_scale(pair_field, conv_gain[layer_index])).astype(jnp.bfloat16)
        padded = extended(activated, (("seq", 0), ("band", 1)), 2 * spread)
        padded = padded[spread : padded.shape[0] - spread]
        conv_term = shear_conv(padded, conv_kernel[layer_index], spread)
        pair_field = (
            (pair_field.astype(jnp.float32) + conv_term + conv_bias[layer_index]) * tile_valid
        ).astype(jnp.bfloat16)
    contacts = jnp.sum(pair_field.astype(jnp.float32) * contact_weight, axis=-1)
    return (trunk_out, contacts)


def solution(mesh):
    return jax.shard_map(
        local,
        mesh=mesh,
        in_specs=(
            P("seq", "band"),
            P("seq"),
            P(),
            P(None, "band"),
            P(None, "band"),
            P(None, "band"),
            P("band", None),
            P(),
            P(),
            P(),
            P(),
            P(),
            P(),
        ),
        out_specs=(P("seq", "band"), P("seq", "band")),
        check_vma=False,
    )
```

profile of v0, /device:TPU:1, one launch (start us, length us, event | category | flops | bytes accessed | tf_op | source)
XLA Modules:
  0.0 434.4 jit_solution(7441531402315791843)
XLA Ops:
  7.2 28.0 %all_gather.12 = bf16[128,1024]{1,0:T(8,128)(2,1)S(1)} all-gather(bf16[128,128]{1,0:T(8,128)(2,1)} %param.13), channel_id=1, replica_groups=mesh['seq'=32,'band'=8] {'band'}, dimensions={1}, use_global_device_ids=true | all-gather | bytes 294912 | tf_op jit(solution)/shard_map/all_gather | solution.py:89
  35.4 1.9 convolution_convert_fusion.4
  37.3 1.9 convolution_convert_fusion.3
  39.3 0.7 convert_bitcast_fusion
  39.9 42.4 %all-gather = bf16[32,1,128]{2,1,0:T(2,128)(2,1)S(1)} all-gather(bf16[1,1,128]{2,1,0:T(2,128)(2,1)S(1)} %convert_bitcast_fusion), channel_id=1, replica_groups=mesh['seq'=32,'band'=8] {'seq'}, dimensions={0}, use_global_device_ids=true | all-gather | bytes 8448 | tf_op jit(solution)/shard_map/all_gather | solution.py:101
  82.4 25.3 %all-gather.4.cloned.1.call-done = bf16[4096,128]{1,0:T(8,128)(2,1)} async-done(((bf16[128,128]{1,0:T(8,128)(2,1)}), bf16[4096,128]{1,0:T(8,128)(2,1)}) %all-gather.4.cloned.1.call-update) | async-done | bytes 1048592 | tf_op jit(solution)/shard_map/all_gather | solution.py:99
  107.6 2.0 fusion.60
  110.1 63.3 %all-gather.6.cloned.1.call-done = bf16[4096,128]{1,0:T(8,128)(2,1)} async-done(((bf16[128,128]{1,0:T(8,128)(2,1)}), bf16[4096,128]{1,0:T(8,128)(2,1)}) %all-gather.6.cloned.1.call-update) | async-done | bytes 1048592 | tf_op jit(solution)/shard_map/all_gather | solution.py:100
  173.4 2.0 convolution_convert_fusion
  175.4 0.8 copy.26
  176.4 73.0 %reduce-scatter.4.cloned.1.call-done = bf16[128,128]{1,0:T(8,128)(2,1)} async-done(((bf16[1024,128]{1,0:T(8,128)(2,1)}), bf16[128,128]{1,0:T(8,128)(2,1)}) %reduce-scatter.4.cloned.1.call-update) | async-done | bytes 32784
  249.5 0.9 copy.27
  250.4 1.5 convolution_convert_fusion.1
  251.9 1.5 convolution_convert_fusion.2
  253.4 84.2 %all-reduce.3.cloned.1.call-done = (bf16[128,128]{1,0:T(8,128)(2,1)}, bf16[128,128]{1,0:T(8,128)(2,1)}) async-done(((bf16[128,128]{1,0:T(8,128)(2,1)}, bf16[128,128]{1,0:T(8,128)(2,1)}), (bf16[128,128]{1,0:T(8,128)(2,1)}, bf16[128,128]{1,0:T(8,128)(2,1)})) %all-reduce.3.cloned.1.call-update) | async-done | bytes 65552 | tf_op jit(solution)/shard_map/psum | solution.py:140
  337.7 0.9 multiply_convert_fusion.1
  338.5 7.8 %collective-permute-start = (bf16[128,128]{1,0:T(8,128)(2,1)S(1)}, bf16[128,128]{1,0:T(8,128)(2,1)S(1)}, u32[]{:S(2)}, u32[]{:S(2)}) collective-permute-start(bf16[128,128]{1,0:T(8,128)(2,1)S(1)} %get-tuple-element.38), channel_id=1, source_target_pairs={{8,0},{16,8},{24,16},{32,24},{40,32},{48,40},{56,48},{64,56},{72,6... | collective-permute-start | bytes 98312 | tf_op jit(solution)/shard_map/ppermute | solution.py:17
  346.4 2.7 collective-permute-done
  349.1 1.9 collective-permute-start.1
  351.0 3.6 collective-permute-done.1
  354.8 0.7 tile.4
  355.5 2.7 slice.172
  358.2 7.7 %reshape.195 = bf16[128,161,128]{2,1,0:T(8,128)(2,1)} reshape(bf16[20608,128]{1,0:T(8,128)(2,1)} %slice.172) | data formatting | bytes 10551296 | tf_op jit(solution)/shard_map/reshape | solution.py:165
  365.9 1.3 slice.173
  367.2 1.9 fusion.1
  369.1 1.5 fusion.5
  370.7 1.9 collective-permute-start.2
  372.6 2.4 collective-permute-start.3
  375.0 2.6 collective-permute-done.3
  377.7 1.3 collective-permute-start.5
  379.0 1.5 collective-permute-start.4
  380.9 4.8 %collective-permute-done.4 = bf16[132,2,128]{2,0,1:T(8,128)(2,1)S(1)} collective-permute-done((bf16[132,2,128]{2,0,1:T(8,128)(2,1)S(1)}, bf16[132,2,128]{2,0,1:T(8,128)(2,1)S(1)}, u32[]{:S(2)}, u32[]{:S(2)}) %collective-permute-start.4) | collective-permute-done | bytes 67616 | tf_op jit(solution)/shard_map/ppermute | solution.py:28
  385.7 0.5 maximum_maximum_fusion.1
  386.7 0.5 slice_dynamic-update-slice_fusion.10
  387.7 1.9 constant_dynamic-update-slice_fusion
  391.1 0.7 fusion.35
  391.8 3.6 fusion.14
  395.4 1.1 fusion.18
  396.5 3.2 collective-permute-start.6
  399.7 1.9 collective-permute-start.7
  401.6 3.3 collective-permute-done.7
  405.0 6.4 %collective-permute-start.9 = (bf16[136,4,128]{2,0,1:T(8,128)(2,1)S(1)}, bf16[136,4,128]{2,0,1:T(8,128)(2,1)S(1)}, u32[]{:S(2)}, u32[]{:S(2)}) collective-permute-start(bf16[136,4,128]{2,0,1:T(8,128)(2,1)S(1)} %get-tuple-element.21), channel_id=1, source_target_pairs={{0,1},{1,2},{2,3},{3,4},{4,5},{5,6},{6,7},{8,9},{9,10},{10,11},{11... | collective-permute-start | bytes 417800 | tf_op jit(solution)/shard_map/ppermute | solution.py:27
  411.4 1.5 collective-permute-start.8
  413.4 5.4 %collective-permute-done.8 = bf16[136,4,128]{2,0,1:T(8,128)(2,1)S(1)} collective-permute-done((bf16[136,4,128]{2,0,1:T(8,128)(2,1)S(1)}, bf16[136,4,128]{2,0,1:T(8,128)(2,1)S(1)}, u32[]{:S(2)}, u32[]{:S(2)}) %collective-permute-start.8) | collective-permute-done | bytes 139296 | tf_op jit(solution)/shard_map/ppermute | solution.py:28
  419.8 0.5 slice_dynamic-update-slice_fusion.4
  420.8 1.4 constant_dynamic-update-slice_fusion.1
  423.7 0.7 fusion.33
  424.4 3.5 multiply_reduce_fusion
  (66 shorter events, 7.6 us)
Async XLA Ops:
  7.2 100.5 %copy-start = (bf16[1024,128]{1,0:T(8,128)(2,1)S(1)}, bf16[1024,128]{1,0:T(8,128)(2,1)}, u32[]{:S(2)}) copy-start(bf16[1024,128]{1,0:T(8,128)(2,1)} %param.16) | copy-start | bytes 786436
  7.2 100.5 %all-gather.4.cloned.1.call-start = ((), (), s32[]{:S(2)}) async-start(), calls=%async_computation.1 | async-start | bytes 1081344 | tf_op jit(solution)/shard_map/all_gather | solution.py:99
  37.3 136.1 %all-gather.6.cloned.1.call-start = ((), (), s32[]{:S(2)}) async-start(), calls=%async_computation.2 | async-start | bytes 1081344 | tf_op jit(solution)/shard_map/all_gather | solution.py:100
  39.2 210.3 %reduce-scatter.4.cloned.1.call-start = ((), (), s32[]{:S(2)}) async-start(), calls=%async_computation.3 | async-start | bytes 294912
  107.6 65.8 %copy-start.3 = (bf16[128,1024]{1,0:T(8,128)(2,1)S(1)}, bf16[128,1024]{1,0:T(8,128)(2,1)}, u32[]{:S(2)}) copy-start(bf16[128,1024]{1,0:T(8,128)(2,1)} %param.19) | copy-start | bytes 786436
  173.4 2.9 copy-start.7
  173.4 3.0 copy-start.1
  173.4 76.9 %copy-start.4 = (bf16[128,128]{1,0:T(8,128)(2,1)S(1)}, bf16[128,128]{1,0:T(8,128)(2,1)}, u32[]{:S(2)}) copy-start(bf16[128,128]{1,0:T(8,128)(2,1)} %param.13) | copy-start | bytes 98308
  175.4 175.6 %copy-start.5 = (f32[2,128]{1,0:T(2,128)S(1)}, f32[2,128]{1,0:T(2,128)}, u32[]{:S(2)}) copy-start(f32[2,128]{1,0:T(2,128)} %param.22) | copy-start | bytes 3076
  176.2 161.4 %all-reduce.3.cloned.1.call-start = ((), (), s32[]{:S(2)}) async-start(), calls=%async_computation.4 | async-start | bytes 131072 | tf_op jit(solution)/shard_map/psum | solution.py:140
  250.4 105.1 %copy-start.2 = (bf16[128,128]{1,0:T(8,128)(2,1)}, bf16[128,128]{1,0:T(8,128)(2,1)S(1)}, u32[]{:S(2)}) copy-start(bf16[128,128]{1,0:T(8,128)(2,1)S(1)} %add_convert_fusion) | copy-start | bytes 98308
  338.5 10.5 %collective-permute-start = (bf16[128,128]{1,0:T(8,128)(2,1)S(1)}, bf16[128,128]{1,0:T(8,128)(2,1)S(1)}, u32[]{:S(2)}, u32[]{:S(2)}) collective-permute-start(bf16[128,128]{1,0:T(8,128)(2,1)S(1)} %get-tuple-element.38), channel_id=1, source_target_pairs={{8,0},{16,8},{24,16},{32,24},{40,32},{48,40},{56,48},{64,56},{72,6... | collective-permute-start | bytes 98312 | tf_op jit(solution)/shard_map/ppermute | solution.py:17
  349.1 5.6 %collective-permute-start.1 = (bf16[256,128]{1,0:T(8,128)(2,1)S(1)}, bf16[256,128]{1,0:T(8,128)(2,1)S(1)}, u32[]{:S(2)}, u32[]{:S(2)}) collective-permute-start(bf16[256,128]{1,0:T(8,128)(2,1)S(1)} %pad_maximum_fusion.9), channel_id=1, source_target_pairs={{8,0},{16,8},{24,16},{32,24},{40,32},{48,40},{56,48},{64,56},{72,6... | collective-permute-start | bytes 196616 | tf_op jit(solution)/shard_map/while/body/eval_jaxpr/ppermute | solution.py:17
  367.2 7.8 %copy-start.6 = (f32[2,128]{1,0:T(2,128)S(1)}, f32[2,128]{1,0:T(2,128)}, u32[]{:S(2)}) copy-start(f32[2,128]{1,0:T(2,128)} %param.24) | copy-start | bytes 3076
  370.7 4.4 %collective-permute-start.2 = (bf16[2,32,128]{2,0,1:T(2,128)(2,1)S(1)}, bf16[2,32,128]{2,0,1:T(2,128)(2,1)S(1)}, u32[]{:S(2)}, u32[]{:S(2)}) collective-permute-start(bf16[2,32,128]{2,0,1:T(2,128)(2,1)S(1)} %get-tuple-element.30), channel_id=1, source_target_pairs={{0,8},{8,16},{16,24},{24,32},{32,40},{40,48},{48,56},{56,64},{64,7... | collective-permute-start | bytes 49160 | tf_op jit(solution)/shard_map/ppermute | solution.py:27
  372.6 5.1 %collective-permute-start.3 = (bf16[2,32,128]{2,0,1:T(2,128)(2,1)S(1)}, bf16[2,32,128]{2,0,1:T(2,128)(2,1)S(1)}, u32[]{:S(2)}, u32[]{:S(2)}) collective-permute-start(bf16[2,32,128]{2,0,1:T(2,128)(2,1)S(1)} %get-tuple-element.29), channel_id=1, source_target_pairs={{8,0},{16,8},{24,16},{32,24},{40,32},{48,40},{56,48},{64,56},{72,6... | collective-permute-start | bytes 49160 | tf_op jit(solution)/shard_map/ppermute | solution.py:28
  377.7 3.1 collective-permute-start.5
  379.0 6.7 %collective-permute-start.4 = (bf16[132,2,128]{2,0,1:T(8,128)(2,1)S(1)}, bf16[132,2,128]{2,0,1:T(8,128)(2,1)S(1)}, u32[]{:S(2)}, u32[]{:S(2)}) collective-permute-start(bf16[132,2,128]{2,0,1:T(8,128)(2,1)S(1)} %get-tuple-element.26), channel_id=1, source_target_pairs={{1,0},{2,1},{3,2},{4,3},{5,4},{6,5},{7,6},{9,8},{10,9},{11,10},{12... | collective-permute-start | bytes 202760 | tf_op jit(solution)/shard_map/ppermute | solution.py:28
  396.5 5.1 %collective-permute-start.6 = (bf16[4,32,128]{2,0,1:T(4,128)(2,1)S(1)}, bf16[4,32,128]{2,0,1:T(4,128)(2,1)S(1)}, u32[]{:S(2)}, u32[]{:S(2)}) collective-permute-start(bf16[4,32,128]{2,0,1:T(4,128)(2,1)S(1)} %get-tuple-element.28), channel_id=1, source_target_pairs={{0,8},{8,16},{16,24},{24,32},{32,40},{40,48},{48,56},{56,64},{64,7... | collective-permute-start | bytes 98312 | tf_op jit(solution)/shard_map/ppermute | solution.py:27
  399.7 5.2 %collective-permute-start.7 = (bf16[4,32,128]{2,0,1:T(4,128)(2,1)S(1)}, bf16[4,32,128]{2,0,1:T(4,128)(2,1)S(1)}, u32[]{:S(2)}, u32[]{:S(2)}) collective-permute-start(bf16[4,32,128]{2,0,1:T(4,128)(2,1)S(1)} %get-tuple-element.27), channel_id=1, source_target_pairs={{8,0},{16,8},{24,16},{32,24},{40,32},{48,40},{56,48},{64,56},{72,6... | collective-permute-start | bytes 98312 | tf_op jit(solution)/shard_map/ppermute | solution.py:28
  405.0 8.4 %collective-permute-start.9 = (bf16[136,4,128]{2,0,1:T(8,128)(2,1)S(1)}, bf16[136,4,128]{2,0,1:T(8,128)(2,1)S(1)}, u32[]{:S(2)}, u32[]{:S(2)}) collective-permute-start(bf16[136,4,128]{2,0,1:T(8,128)(2,1)S(1)} %get-tuple-element.21), channel_id=1, source_target_pairs={{0,1},{1,2},{2,3},{3,4},{4,5},{5,6},{6,7},{8,9},{9,10},{10,11},{11... | collective-permute-start | bytes 417800 | tf_op jit(solution)/shard_map/ppermute | solution.py:27
  411.4 7.4 %collective-permute-start.8 = (bf16[136,4,128]{2,0,1:T(8,128)(2,1)S(1)}, bf16[136,4,128]{2,0,1:T(8,128)(2,1)S(1)}, u32[]{:S(2)}, u32[]{:S(2)}) collective-permute-start(bf16[136,4,128]{2,0,1:T(8,128)(2,1)S(1)} %get-tuple-element.22), channel_id=1, source_target_pairs={{1,0},{2,1},{3,2},{4,3},{5,4},{6,5},{7,6},{9,8},{10,9},{11,10},{12... | collective-permute-start | bytes 417800 | tf_op jit(solution)/shard_map/ppermute | solution.py:28
  423.2 1.2 copy-start.8
Sparse Core Ops, SparseCore 0:
  37.4 70.2 all-gather.3
  110.1 63.2 all-gather.5
  177.2 72.2 reduce-scatter.3
  253.5 84.0 all-reduce.2
where the time goes:
time: 439 us; the launch traced here: 434 us
  waiting for transfers between devices  268 us (61%)
  blocking collectives  70.4 us (16%)
  starting transfers between devices  29.9 us (7%)
  local copies, waits for them, and re-layouts  20.2 us (5%)
  matrix products  17.8 us (4%)
  between operations  14.3 us (3%)
  other arithmetic  13.3 us (3%)
    psum x1, waiting for transfers between devices, local(): lax.psum(jnp.dot(trunk_out, rows_right, preferred_element_type=jnp.float3...  84.2 us
    unnamed x5, waiting for transfers between devices  73.1 us
    all_gather x1, waiting for transfers between devices, local(): value_piece = lax.all_gather(value, 'seq', axis=0, tiled=True)  63.3 us
    all_gather x1, blocking collectives, local(): offset_piece = lax.all_gather(key_offset, 'seq', axis=0, tiled=True)  42.4 us
    all_gather x1, blocking collectives, local(): gathered = lax.all_gather(tokens, 'band', axis=1, tiled=True)  28 us
    all_gather x1, waiting for transfers between devices, local(): key_piece = lax.all_gather(key_rows, 'seq', axis=0, tiled=True)  25.3 us
    ppermute x4, waiting for transfers between devices, extended(): after = lax.ppermute(initial, axis, down)  16.1 us
    ppermute x4, starting transfers between devices, extended(): before = lax.ppermute(last, axis, up)  12.8 us
  transfers between devices with their start and end apart: 14, of which 11 were waited for; matrix products, arithmetic and copies ran while one was open for 1% of the time, Pallas kernels for 0%

commit v1 on v0

v1 whole, which is shorter than its diff:
```python
import jax
import jax.numpy as jnp
from jax import lax
from jax.experimental import pallas as pl
from jax.experimental.pallas import tpu as pltpu
from jax.sharding import PartitionSpec as P

HEAD = 128
DIAG = 32
BINS = 128
EPS = 1e-06
BANDS = 8
RING = 8
SEQ = 32
MESH = pl.DeviceIdType.MESH
F32 = jnp.float32
BF16 = jnp.bfloat16


def remote(src, dst, send_sem, recv_sem, **device):
    return pltpu.make_async_remote_copy(
        src_ref=src,
        dst_ref=dst,
        send_sem=send_sem,
        recv_sem=recv_sem,
        device_id=device,
        device_id_type=MESH,
    )


def trunk_kernel(
    tok_ref,
    map_ref,
    gain_ref,
    wq_ref,
    wk_ref,
    wv_ref,
    wout_ref,
    wl_ref,
    wr_ref,
    trunk_ref,
    left_ref,
    right_ref,
    tok_all,
    wqkv,
    wout,
    wlr,
    m_all,
    wcol_all,
    q_all,
    kv,
    o_send,
    o_recv,
    st_send,
    st_recv,
    att_all,
    leftbuf,
    rightbuf,
    local_sem,
    tok_s,
    tok_r,
    m_s,
    m_r,
    wc_s,
    wc_r,
    q_s,
    q_r,
    kv_s,
    kv_r,
    o_s,
    o_r,
    st_s,
    st_r,
    att_s,
    att_r,
    edge_s,
    edge_r,
):
    seq = lax.axis_index("seq")
    band = lax.axis_index("band")
    core = seq % 2
    ring = (seq // 2) % RING
    half = seq // (2 * RING)

    def seq_of(half_, ring_, core_):
        return half_ * (2 * RING) + ring_ * 2 + core_

    up = seq_of(half, (ring + 1) % RING, core)
    down = seq_of(half, (ring + RING - 1) % RING, core)
    mates = [
        None,
        seq_of(half, ring, 1 - core),
        seq_of(1 - half, ring, core),
        seq_of(1 - half, ring, 1 - core),
    ]
    near = {k: (seq + SEQ + k) % SEQ for k in (-3, -2, -1, 1, 2, 3)}

    def to_band(k):
        return (band + k) % BANDS

    def from_band(k):
        return (band + BANDS - k) % BANDS

    loads = [
        pltpu.make_async_copy(wout_ref, wout, local_sem.at[0]),
        pltpu.make_async_copy(wl_ref, wlr.at[:, pl.ds(0, 128)], local_sem.at[1]),
        pltpu.make_async_copy(wr_ref, wlr.at[:, pl.ds(128, 128)], local_sem.at[2]),
        pltpu.make_async_copy(wq_ref, wqkv.at[:, pl.ds(0, 128)], local_sem.at[3]),
        pltpu.make_async_copy(wk_ref, wqkv.at[:, pl.ds(128, 128)], local_sem.at[4]),
        pltpu.make_async_copy(wv_ref, wqkv.at[:, pl.ds(256, 128)], local_sem.at[5]),
    ]
    for load in loads:
        load.start()

    barrier = pltpu.get_barrier_semaphore()
    greeted = 0
    for k in range(1, BANDS):
        pl.semaphore_signal(barrier, inc=1, device_id={"band": to_band(k)}, device_id_type=MESH)
        greeted += 1
    for other in [up, down] + mates[1:] + list(near.values()):
        pl.semaphore_signal(barrier, inc=1, device_id={"seq": other}, device_id_type=MESH)
        greeted += 1
    pl.semaphore_wait(barrier, greeted)

    def band_send(src, dst_all, s_sem, r_sem, k):
        return remote(src, dst_all.at[band], s_sem.at[k], r_sem.at[k], band=to_band(k))

    def band_recv(dst_all, s_sem, r_sem, k):
        slot = dst_all.at[from_band(k)]
        return remote(slot, slot, s_sem.at[k], r_sem.at[k], band=to_band(k))

    tok_sends = [band_send(tok_ref, tok_all, tok_s, tok_r, k) for k in range(1, BANDS)]
    for send in tok_sends:
        send.start()
    tok_all[band] = tok_ref[...]

    for load in loads:
        load.wait()
    m_all[band] = jnp.dot(wout[...], wlr[...], preferred_element_type=F32).astype(BF16)
    for k in range(1, BANDS):
        band_recv(tok_all, tok_s, tok_r, k).wait_recv()

    floats = jnp.concatenate([tok_all[c] for c in range(BANDS)], axis=1).astype(F32)
    inv = lax.rsqrt(jnp.mean(floats * floats, axis=-1, keepdims=True) + EPS)
    normed = (floats * inv * gain_ref[...]).astype(BF16)
    qkv = jnp.dot(normed, wqkv[...], preferred_element_type=F32)
    offset = ((map_ref[...] - 1).astype(F32) * 1000000000.0).astype(BF16)
    q_all[0] = qkv[:, 0:128].astype(BF16)
    kv[0, 0:128] = qkv[:, 128:256].astype(BF16)
    kv[0, 128:256] = qkv[:, 256:384].T.astype(BF16)
    kv[0, 256:272] = jnp.broadcast_to(offset, (16, 128))

    def kv_copy(src, dst, sem, other):
        return remote(kv.at[src], kv.at[dst], kv_s.at[sem], kv_r.at[dst], seq=other)

    kv_sends = [kv_copy(0, 1, 0, up), kv_copy(0, 7, 4, down)]
    for send in kv_sends:
        send.start()
    q_copies = [
        remote(q_all.at[0], q_all.at[k], q_s.at[k], q_r.at[k], seq=mates[k]) for k in (1, 2, 3)
    ]
    for copy in q_copies:
        copy.start()
    m_sends = [band_send(m_all.at[band], m_all, m_s, m_r, k) for k in range(1, BANDS)]
    wc_sends = [
        band_send(
            wout.at[:, pl.ds(pl.multiple_of(to_band(k) * 128, 128), 128)], wcol_all, wc_s, wc_r, k
        )
        for k in range(1, BANDS)
    ]
    for send in m_sends + wc_sends:
        send.start()
    wcol_all[band] = wout[:, pl.ds(pl.multiple_of(band * 128, 128), 128)]
    lr_tok = jnp.dot(floats.astype(BF16), wlr[...], preferred_element_type=F32)
    for copy in q_copies:
        copy.wait_recv()
    queries = jnp.concatenate([q_all[k] for k in range(4)], axis=0)

    def attend(state, slots):
        keys = jnp.concatenate([kv[j, 0:128] for j in slots], axis=0)
        values_t = jnp.concatenate([kv[j, 128:256] for j in slots], axis=1)
        offs = jnp.concatenate(
            [
                jnp.broadcast_to(kv[j, 256:272][0:1].astype(F32), (128, 128)).T
                for j in slots
            ],
            axis=0,
        )
        offs = jnp.concatenate([offs] * 4, axis=1)
        scores = (
            lax.dot_general(
                keys, queries, (((1,), (1,)), ((), ())), preferred_element_type=F32
            )
            * HEAD ** (-0.5)
            + offs
        )
        block_top = jnp.max(scores, axis=0, keepdims=True)
        if state is None:
            top = block_top
        else:
            top = jnp.maximum(state[0], block_top)
        weights = jnp.exp(scores - top)
        block_sum = jnp.sum(weights, axis=0, keepdims=True)
        mixed = jnp.dot(values_t, weights.astype(BF16), preferred_element_type=F32)
        if state is None:
            return top, block_sum, mixed
        fade = jnp.exp(state[0] - top)
        return top, state[1] * fade + block_sum, state[2] * fade + mixed

    state = attend(None, [0])
    for t in (1, 2, 3, 4):
        kv_copy(t, t, t, up).wait_recv()
        if t < 4:
            send = kv_copy(t, t + 1, t, up)
            send.start()
            kv_sends.append(send)
            low = RING - t
            kv_copy(low, low, t, down).wait_recv()
            if t < 3:
                send = kv_copy(low, low - 1, 4 + t, down)
                send.start()
                kv_sends.append(send)
            state = attend(state, [t, low])
        else:
            state = attend(state, [t])

    top, total, mixed = state
    mixed = mixed / total
    o_copies = []
    for k in (1, 2, 3):
        lanes = slice(k * 128, (k + 1) * 128)
        o_send[k] = mixed[:, lanes].astype(BF16)
        st_send[k, 0:4] = jnp.broadcast_to(top[:, lanes], (4, 128))
        st_send[k, 4:8] = jnp.broadcast_to(total[:, lanes], (4, 128))
        o_copies.append(
            remote(st_send.at[k], st_recv.at[k], st_s.at[k], st_r.at[k], seq=mates[k])
        )
        o_copies.append(remote(o_send.at[k], o_recv.at[k], o_s.at[k], o_r.at[k], seq=mates[k]))
    for copy in o_copies:
        copy.start()
    keep = jnp.broadcast_to(map_ref[...].astype(F32), (128, 128)).T
    keep = jnp.concatenate([keep, keep], axis=1)
    for copy in o_copies:
        copy.wait_recv()
    tops = [top[:, 0:128]] + [st_recv[k, 0:1] for k in (1, 2, 3)]
    sums = [total[:, 0:128]] + [st_recv[k, 4:5] for k in (1, 2, 3)]
    parts = [mixed[:, 0:128]] + [o_recv[k].astype(F32) for k in (1, 2, 3)]
    best = jnp.maximum(jnp.maximum(tops[0], tops[1]), jnp.maximum(tops[2], tops[3]))
    shares = [s * jnp.exp(t - best) for s, t in zip(sums, tops)]
    share_sum = shares[0] + shares[1] + shares[2] + shares[3]
    attended = (
        parts[0] * shares[0] + parts[1] * shares[1] + parts[2] * shares[2] + parts[3] * shares[3]
    ) / share_sum
    att_all[band] = attended.T.astype(BF16)
    att_sends = [band_send(att_all.at[band], att_all, att_s, att_r, k) for k in range(1, BANDS)]
    for send in att_sends:
        send.start()
    for k in range(1, BANDS):
        band_recv(m_all, m_s, m_r, k).wait_recv()
        band_recv(wcol_all, wc_s, wc_r, k).wait_recv()
    for k in range(1, BANDS):
        band_recv(att_all, att_s, att_r, k).wait_recv()

    heads = jnp.concatenate([att_all[c] for c in range(BANDS)], axis=1)
    both = lr_tok + jnp.dot(
        heads, m_all[...].reshape(BANDS * 128, 256), preferred_element_type=F32
    )
    both = (both * keep).astype(BF16)
    leftbuf[16:144] = both[:, 0:128]
    rightbuf[16:144] = both[:, 128:256]

    def edge(src, dst, sem, other):
        return remote(src, dst, edge_s.at[sem], edge_r.at[sem], seq=other)

    own = rightbuf.at[pl.ds(16, 128)]
    edges = [
        edge(own, rightbuf.at[pl.ds(144, 128)], 0, near[-1]),
        edge(own, rightbuf.at[pl.ds(272, 128)], 1, near[-2]),
        edge(rightbuf.at[pl.ds(16, 16)], rightbuf.at[pl.ds(400, 16)], 2, near[-3]),
        edge(rightbuf.at[pl.ds(128, 16)], rightbuf.at[pl.ds(0, 16)], 3, near[1]),
        edge(leftbuf.at[pl.ds(16, 16)], leftbuf.at[pl.ds(144, 16)], 4, near[-1]),
        edge(leftbuf.at[pl.ds(128, 16)], leftbuf.at[pl.ds(0, 16)], 5, near[1]),
    ]
    for copy in edges:
        copy.start()
    summed = jnp.dot(
        heads, wcol_all[...].reshape(BANDS * 128, 128), preferred_element_type=F32
    )
    trunk_ref[...] = (tok_ref[...].astype(F32) + summed).astype(BF16)
    for copy in edges:
        copy.wait_recv()
    left_ref[...] = leftbuf[...]
    right_ref[...] = rightbuf[pl.ds(pl.multiple_of(band * DIAG, DIAG), 192)]
    for send in tok_sends + kv_sends + q_copies + m_sends + wc_sends + o_copies:
        send.wait_send()
    for send in att_sends + edges:
        send.wait_send()


ROWS = 144
LEAD = 8
WIDE0 = 44
WIDE1 = 40
GROUP = 4


def gelu_norm(field, gain):
    inv = lax.rsqrt(jnp.mean(field * field, axis=-1, keepdims=True) + EPS)
    x = field * inv * gain
    inner = x * (0.7978845608028654 + 0.035677408136300125 * (x * x))
    return (0.5 * x) * (1.0 + jnp.tanh(inner))


def map_kernel(
    left_ref,
    right_ref,
    gain_ref,
    kern_ref,
    bias_ref,
    weight_ref,
    out_ref,
    lf,
    rf,
    act0,
    field1,
    act1,
):
    seq = lax.axis_index("seq")
    band = lax.axis_index("band")
    length = SEQ * BINS
    lf[...] = left_ref[...].astype(F32)
    rf[...] = right_ref[...].astype(F32)
    place = lax.broadcasted_iota(jnp.int32, (ROWS, 128), 0)
    first = seq * BINS - LEAD

    def bounds(diag):
        known = (diag >= 0) & (diag < BANDS * DIAG)
        low = -first
        high = jnp.minimum(length, length - diag) - first
        return low, jnp.where(known, high, low)

    def masked(value, diag):
        low, high = bounds(diag)
        return jnp.where((place >= low) & (place < high), value, 0.0)

    def start_field(delta):
        value = lf[LEAD : LEAD + ROWS] * rf[pl.ds(delta + 2, ROWS)]
        return masked(value, band * DIAG + delta - 6).astype(BF16).astype(F32)

    gain0 = gain_ref[0:1]
    gain1 = gain_ref[1:2]

    @pl.loop(0, WIDE0)
    def _(delta):
        act = gelu_norm(start_field(delta), gain0)
        act0[0, delta] = pltpu.roll(act, 1, 0).astype(BF16)
        act0[1, delta] = act.astype(BF16)
        act0[2, delta] = pltpu.roll(act, ROWS - 1, 0).astype(BF16)

    @pl.loop(0, WIDE1 // GROUP)
    def _(step):
        diag = step * GROUP
        taps = jnp.concatenate(
            [
                act0[p, pl.ds(diag + 2 + q - p, GROUP)].reshape(GROUP * ROWS, 128)
                for p in range(3)
                for q in range(3)
            ],
            axis=1,
        )
        term = jnp.dot(taps, kern_ref[0], preferred_element_type=F32)
        for g in range(GROUP):
            value = term[g * ROWS : (g + 1) * ROWS] + start_field(diag + g + 2) + bias_ref[0:1]
            value = masked(value, band * DIAG + diag + g - 4).astype(BF16)
            field1[diag + g] = value
            act = gelu_norm(value.astype(F32), gain1)
            act1[0, diag + g] = pltpu.roll(act, 2, 0)[LEAD : LEAD + BINS].astype(BF16)
            act1[1, diag + g] = act[LEAD : LEAD + BINS].astype(BF16)
            act1[2, diag + g] = pltpu.roll(act, ROWS - 2, 0)[LEAD : LEAD + BINS].astype(BF16)

    lane = lax.broadcasted_iota(jnp.int32, (BINS, 128), 1)
    spot = lax.broadcasted_iota(jnp.int32, (BINS, 128), 0) + seq * BINS

    def last(step, found):
        diag = step * GROUP
        taps = jnp.concatenate(
            [
                act1[p, pl.ds(diag + 4 + 2 * (q - p), GROUP)].reshape(GROUP * BINS, 128)
                for p in range(3)
                for q in range(3)
            ],
            axis=1,
        )
        term = jnp.dot(taps, kern_ref[1], preferred_element_type=F32)
        for g in range(GROUP):
            value = (
                term[g * BINS : (g + 1) * BINS]
                + field1[diag + g + 4].astype(F32)[LEAD : LEAD + BINS]
                + bias_ref[1:2]
            )
            value = jnp.where(spot + (band * DIAG + diag + g) < length, value, 0.0)
            value = value.astype(BF16).astype(F32)
            contact = jnp.sum(value * weight_ref[...], axis=-1, keepdims=True)
            found = jnp.where(lane == diag + g, contact, found)
        return found

    found = lax.fori_loop(0, DIAG // GROUP, last, jnp.zeros((BINS, 128), F32))
    out_ref[...] = found[:, 0:DIAG]


def local(
    tokens,
    mappable,
    attn_gain,
    w_query,
    w_key,
    w_value,
    w_out,
    w_left,
    w_right,
    conv_gain,
    conv_kernel,
    conv_bias,
    contact_weight,
):
    vmem = pl.BlockSpec(memory_space=pltpu.VMEM)
    anywhere = pl.BlockSpec(memory_space=pl.ANY)
    dma = pltpu.SemaphoreType.DMA
    trunk_out, left, right = pl.pallas_call(
        trunk_kernel,
        out_shape=(
            jax.ShapeDtypeStruct((BINS, 128), BF16),
            jax.ShapeDtypeStruct((160, 128), BF16),
            jax.ShapeDtypeStruct((192, 128), BF16),
        ),
        in_specs=[vmem] * 3 + [anywhere] * 6,
        out_specs=(vmem, vmem, vmem),
        scratch_shapes=[
            pltpu.VMEM((BANDS, 128, 128), BF16),
            pltpu.VMEM((1024, 384), BF16),
            pltpu.VMEM((128, 1024), BF16),
            pltpu.VMEM((1024, 256), BF16),
            pltpu.VMEM((BANDS, 128, 256), BF16),
            pltpu.VMEM((BANDS, 128, 128), BF16),
            pltpu.VMEM((4, 128, 128), BF16),
            pltpu.VMEM((RING, 272, 128), BF16),
            pltpu.VMEM((4, 128, 128), BF16),
            pltpu.VMEM((4, 128, 128), BF16),
            pltpu.VMEM((4, 8, 128), F32),
            pltpu.VMEM((4, 8, 128), F32),
            pltpu.VMEM((BANDS, 128, 128), BF16),
            pltpu.VMEM((160, 128), BF16),
            pltpu.VMEM((416, 128), BF16),
            dma((6,)),
        ]
        + [dma((8,)) for _ in range(18)],
        compiler_params=pltpu.CompilerParams(
            collective_id=0, has_side_effects=True, vmem_limit_bytes=32 * 1024 * 1024
        ),
    )(
        tokens,
        mappable.reshape(1, BINS),
        attn_gain.reshape(1, -1),
        w_query,
        w_key,
        w_value,
        w_out,
        w_left,
        w_right,
    )
    contacts = pl.pallas_call(
        map_kernel,
        out_shape=jax.ShapeDtypeStruct((BINS, DIAG), F32),
        in_specs=[vmem] * 6,
        out_specs=vmem,
        scratch_shapes=[
            pltpu.VMEM((160, 128), F32),
            pltpu.VMEM((192, 128), F32),
            pltpu.VMEM((3, WIDE0, ROWS, 128), BF16),
            pltpu.VMEM((WIDE1, ROWS, 128), BF16),
            pltpu.VMEM((3, WIDE1, BINS, 128), BF16),
        ],
        compiler_params=pltpu.CompilerParams(vmem_limit_bytes=40 * 1024 * 1024),
    )(
        left,
        right,
        conv_gain,
        conv_kernel.reshape(2, 9 * 128, 128),
        conv_bias,
        contact_weight.reshape(1, 128),
    )
    return (trunk_out, contacts)


def solution(mesh):
    return jax.shard_map(
        local,
        mesh=mesh,
        in_specs=(
            P("seq", "band"),
            P("seq"),
            P(),
            P(None, "band"),
            P(None, "band"),
            P(None, "band"),
            P("band", None),
            P(),
            P(),
            P(),
            P(),
            P(),
            P(),
        ),
        out_specs=(P("seq", "band"), P("seq", "band")),
        check_vma=False,
    )
```

time: 439 us -> 76.4 us (0.17)
  waiting for transfers between devices: 268 us -> 0 us
  blocking collectives: 70.4 us -> 0 us
  Pallas kernels: 0 us -> 66.2 us
  starting transfers between devices: 29.9 us -> 0 us
  matrix products: 17.8 us -> 0 us
  between operations: 14.3 us -> 0.71 us
  other arithmetic: 13.3 us -> 0 us
  local copies, waits for them, and re-layouts: 20.2 us -> 9.08 us
    all_gather x2 -> x0, waiting for transfers between devices: 88.5 us -> none  [the longest x1 63.3 us: local(): value_piece = lax.all_gather(value, 'seq', axis=0, tiled=True)]
    psum x1 -> x0, waiting for transfers between devices: 84.2 us -> none  [local(): lax.psum(jnp.dot(trunk_out, rows_right, preferred_element_type=jnp.float3...]
    unnamed x5 -> x0, waiting for transfers between devices: 73.1 us -> none
    all_gather x2 -> x0, blocking collectives: 70.4 us -> none  [the longest x1 42.4 us: local(): offset_piece = lax.all_gather(key_offset, 'seq', axis=0, tiled=True)]
    pallas_call x0 -> x2, Pallas kernels: none -> 66.2 us  [the longest x1 47.4 us: local(): pl.pallas_call(trunk_kernel, out_shape=(jax.ShapeDtypeStruct((BINS, 128),...]
    ppermute x10 -> x0, starting transfers between devices: 29.8 us -> none  [the longest x4 12.8 us: extended(): before = lax.ppermute(last, axis, up)]
    ppermute x10 -> x0, waiting for transfers between devices: 22.5 us -> none  [the longest x4 16.1 us: extended(): after = lax.ppermute(initial, axis, down)]
    dot_general x8 -> x0, matrix products: 17.8 us -> none  [the longest x2 7.07 us: shear_conv(): jnp.einsum('aek,kf->aef', stacked, flat_kernel, preferred_element_type=jn...]
  transfers between devices with their start and end apart: 14 -> 0, of which waited for: 11 -> 0; matrix products, arithmetic and copies ran while one was open for 1% -> 0% of each run, Pallas kernels for 0% -> 0%
where the time goes in v1:
time: 76.4 us; the launch traced here: 76 us
  Pallas kernels  66.2 us (87%)
  local copies, waits for them, and re-layouts  9.08 us (12%)
    pallas_call x1, Pallas kernels, local(): pl.pallas_call(trunk_kernel, out_shape=(jax.ShapeDtypeStruct((BINS, 128),...  47.4 us
    pallas_call x1, Pallas kernels, local(): pl.pallas_call(map_kernel, out_shape=jax.ShapeDtypeStruct((BINS, DIAG), F...  18.8 us
    unnamed x28, local copies, waits for them, and re-layouts  9.08 us

profile of v1, /device:TPU:1, one launch (start us, length us, event | category | flops | bytes accessed | tf_op | source)
XLA Modules:
  0.0 76.0 jit_solution(2717773541609861405)
XLA Ops:
  0.6 0.0 copy-start.8
  0.6 0.0 copy-start.11
  0.7 0.7 copy-done.8
  1.3 0.0 copy-done.11
  1.3 0.0 copy-start.1
  1.3 0.9 %copy-done.1 = bf16[1024,128]{1,0:T(8,128)(2,1)S(1)} copy-done((bf16[1024,128]{1,0:T(8,128)(2,1)S(1)}, bf16[1024,128]{1,0:T(8,128)(2,1)}, u32[]{:S(2)}) %copy-start.1) | copy-done | bytes 262168
  2.3 0.0 copy-start.2
  2.3 0.9 %copy-done.2 = bf16[1024,128]{1,0:T(8,128)(2,1)S(1)} copy-done((bf16[1024,128]{1,0:T(8,128)(2,1)S(1)}, bf16[1024,128]{1,0:T(8,128)(2,1)}, u32[]{:S(2)}) %copy-start.2) | copy-done | bytes 262168
  3.2 0.0 copy-start.3
  3.2 0.9 %copy-done.3 = bf16[1024,128]{1,0:T(8,128)(2,1)S(1)} copy-done((bf16[1024,128]{1,0:T(8,128)(2,1)S(1)}, bf16[1024,128]{1,0:T(8,128)(2,1)}, u32[]{:S(2)}) %copy-start.3) | copy-done | bytes 262168
  4.2 0.0 copy-start.4
  4.2 0.9 %copy-done.4 = bf16[128,1024]{1,0:T(8,128)(2,1)S(1)} copy-done((bf16[128,1024]{1,0:T(8,128)(2,1)S(1)}, bf16[128,1024]{1,0:T(8,128)(2,1)}, u32[]{:S(2)}) %copy-start.4) | copy-done | bytes 262168
  5.1 0.0 copy-start.5
  5.1 0.9 %copy-done.5 = bf16[1024,128]{1,0:T(8,128)(2,1)S(1)} copy-done((bf16[1024,128]{1,0:T(8,128)(2,1)S(1)}, bf16[1024,128]{1,0:T(8,128)(2,1)}, u32[]{:S(2)}) %copy-start.5) | copy-done | bytes 262168
  6.1 0.0 copy-start.6
  6.1 0.9 %copy-done.6 = bf16[1024,128]{1,0:T(8,128)(2,1)S(1)} copy-done((bf16[1024,128]{1,0:T(8,128)(2,1)S(1)}, bf16[1024,128]{1,0:T(8,128)(2,1)}, u32[]{:S(2)}) %copy-start.6) | copy-done | bytes 262168
  7.0 0.0 copy-start.7
  7.0 0.8 copy-done.7
  7.8 0.0 copy-start
  7.8 0.0 copy-start.10
  7.8 47.4 %shard_map.140 = (bf16[128,128]{1,0:T(8,128)(2,1)S(1)}, bf16[160,128]{1,0:T(8,128)(2,1)S(1)}, bf16[192,128]{1,0:T(8,128)(2,1)S(1)}) custom-call(bf16[128,128]{1,0:T(8,128)(2,1)S(1)} %copy-done.7, s32[1,128]{1,0:T(1,128)S(1)} %bitcast.6, f32[1,1024]{1,0:T(1,128)S(1)} %bitcast.5, bf16[1024,128]{1,0:T(8,128)(2,1)S(1)} %copy-done.1, ...), custom_call_target="tpu_custom_call" | custom-call | tf_op jit(solution)/shard_map/pallas_call | solution.py:429
  55.2 0.0 copy-start.9
  55.2 0.0 copy-start.12
  55.3 0.0 copy-done
  55.3 0.0 copy-done.10
  55.3 0.6 copy-done.9
  55.9 0.0 copy-done.12
  55.9 18.8 %shard_map.141 = f32[128,32]{1,0:T(8,128)S(1)} custom-call(bf16[160,128]{1,0:T(8,128)(2,1)S(1)} %get-tuple-element.6.left_ref, bf16[192,128]{1,0:T(8,128)(2,1)S(1)} %get-tuple-element.7.right_ref, f32[2,128]{1,0:T(2,128)S(1)} %copy-done.9, bf16[2,1152,128]{2,1,0:T(8,128)(2,1)S(1)} %bitcast.4, f32[2,128]{1,0:T(2,128)S(1)} %copy-done.10, f32[1,128]{1,0:T(1,128)S(1)} %bitcast.7), custom_call_target="tpu_custom_call" | custom-call | tf_op jit(solution)/shard_map/pallas_call | solution.py:471
  74.7 0.7 copy.15
  75.4 0.6 copy.17
Async XLA Ops:
  0.6 0.7 copy-start.8
  0.6 0.7 copy-start.11
  1.3 1.0 %copy-start.1 = (bf16[1024,128]{1,0:T(8,128)(2,1)S(1)}, bf16[1024,128]{1,0:T(8,128)(2,1)}, u32[]{:S(2)}) copy-start(bf16[1024,128]{1,0:T(8,128)(2,1)} %wq_ref.1) | copy-start | bytes 786436
  2.3 0.9 %copy-start.2 = (bf16[1024,128]{1,0:T(8,128)(2,1)S(1)}, bf16[1024,128]{1,0:T(8,128)(2,1)}, u32[]{:S(2)}) copy-start(bf16[1024,128]{1,0:T(8,128)(2,1)} %wk_ref.1) | copy-start | bytes 786436
  3.2 0.9 %copy-start.3 = (bf16[1024,128]{1,0:T(8,128)(2,1)S(1)}, bf16[1024,128]{1,0:T(8,128)(2,1)}, u32[]{:S(2)}) copy-start(bf16[1024,128]{1,0:T(8,128)(2,1)} %wv_ref.1) | copy-start | bytes 786436
  4.2 0.9 %copy-start.4 = (bf16[128,1024]{1,0:T(8,128)(2,1)S(1)}, bf16[128,1024]{1,0:T(8,128)(2,1)}, u32[]{:S(2)}) copy-start(bf16[128,1024]{1,0:T(8,128)(2,1)} %wout_ref.1) | copy-start | bytes 786436
  5.1 0.9 %copy-start.5 = (bf16[1024,128]{1,0:T(8,128)(2,1)S(1)}, bf16[1024,128]{1,0:T(8,128)(2,1)}, u32[]{:S(2)}) copy-start(bf16[1024,128]{1,0:T(8,128)(2,1)} %wl_ref.1) | copy-start | bytes 786436
  6.1 0.9 %copy-start.6 = (bf16[1024,128]{1,0:T(8,128)(2,1)S(1)}, bf16[1024,128]{1,0:T(8,128)(2,1)}, u32[]{:S(2)}) copy-start(bf16[1024,128]{1,0:T(8,128)(2,1)} %wr_ref.1) | copy-start | bytes 786436
  7.0 0.8 copy-start.7
  7.8 47.5 %copy-start = (bf16[2,3,3,128,128]{4,3,2,1,0:T(8,128)(2,1)S(1)}, bf16[2,3,3,128,128]{4,3,2,1,0:T(8,128)(2,1)}, u32[]{:S(2)}) copy-start(bf16[2,3,3,128,128]{4,3,2,1,0:T(8,128)(2,1)} %param.23) | copy-start | bytes 1769476
  7.8 47.5 %copy-start.10 = (f32[2,128]{1,0:T(2,128)S(1)}, f32[2,128]{1,0:T(2,128)}, u32[]{:S(2)}) copy-start(f32[2,128]{1,0:T(2,128)} %bias_ref.1) | copy-start | bytes 3076
  55.2 0.7 copy-start.9
  55.2 0.7 copy-start.12

commit v2 on v1

--- a/solution.py
+++ b/solution.py
@@ -42,6 +42,8 @@
     left_ref,
     right_ref,
     tok_all,
+    gain_v,
+    map_v,
     wqkv,
     wout,
     wlr,
@@ -108,6 +110,9 @@
         pltpu.make_async_copy(wq_ref, wqkv.at[:, pl.ds(0, 128)], local_sem.at[3]),
         pltpu.make_async_copy(wk_ref, wqkv.at[:, pl.ds(128, 128)], local_sem.at[4]),
         pltpu.make_async_copy(wv_ref, wqkv.at[:, pl.ds(256, 128)], local_sem.at[5]),
+        pltpu.make_async_copy(gain_ref, gain_v, local_sem.at[6]),
+        pltpu.make_async_copy(map_ref, map_v, local_sem.at[7]),
+        pltpu.make_async_copy(tok_ref, tok_all.at[band], local_sem.at[8]),
     ]
     for load in loads:
         load.start()
@@ -132,7 +137,6 @@
     tok_sends = [band_send(tok_ref, tok_all, tok_s, tok_r, k) for k in range(1, BANDS)]
     for send in tok_sends:
         send.start()
-    tok_all[band] = tok_ref[...]
 
     for load in loads:
         load.wait()
@@ -142,9 +146,9 @@
 
     floats = jnp.concatenate([tok_all[c] for c in range(BANDS)], axis=1).astype(F32)
     inv = lax.rsqrt(jnp.mean(floats * floats, axis=-1, keepdims=True) + EPS)
-    normed = (floats * inv * gain_ref[...]).astype(BF16)
+    normed = (floats * inv * gain_v[...]).astype(BF16)
     qkv = jnp.dot(normed, wqkv[...], preferred_element_type=F32)
-    offset = ((map_ref[...] - 1).astype(F32) * 1000000000.0).astype(BF16)
+    offset = ((map_v[...] - 1).astype(F32) * 1000000000.0).astype(BF16)
     q_all[0] = qkv[:, 0:128].astype(BF16)
     kv[0, 0:128] = qkv[:, 128:256].astype(BF16)
     kv[0, 128:256] = qkv[:, 256:384].T.astype(BF16)
@@ -238,7 +242,7 @@
         o_copies.append(remote(o_send.at[k], o_recv.at[k], o_s.at[k], o_r.at[k], seq=mates[k]))
     for copy in o_copies:
         copy.start()
-    keep = jnp.broadcast_to(map_ref[...].astype(F32), (128, 128)).T
+    keep = jnp.broadcast_to(map_v[...].astype(F32), (128, 128)).T
     keep = jnp.concatenate([keep, keep], axis=1)
     for copy in o_copies:
         copy.wait_recv()
@@ -286,7 +290,7 @@
     summed = jnp.dot(
         heads, wcol_all[...].reshape(BANDS * 128, 128), preferred_element_type=F32
     )
-    trunk_ref[...] = (tok_ref[...].astype(F32) + summed).astype(BF16)
+    trunk_ref[...] = (tok_all[band].astype(F32) + summed).astype(BF16)
     for copy in edges:
         copy.wait_recv()
     left_ref[...] = leftbuf[...]
@@ -297,115 +301,192 @@
         send.wait_send()
 
 
-ROWS = 144
+CHUNK = 9
+LANES = 16
+ROWS = CHUNK * LANES
 LEAD = 8
 WIDE0 = 44
 WIDE1 = 40
 GROUP = 4
 
 
-def gelu_norm(field, gain):
-    inv = lax.rsqrt(jnp.mean(field * field, axis=-1, keepdims=True) + EPS)
-    x = field * inv * gain
-    inner = x * (0.7978845608028654 + 0.035677408136300125 * (x * x))
-    return (0.5 * x) * (1.0 + jnp.tanh(inner))
+def norm_gelu(field, half_gain, keep):
+    squares = jnp.sum(field * field, axis=-1, keepdims=True)
+    inv = lax.rsqrt(squares + HEAD * EPS)
+    if keep is not None:
+        inv = jnp.where(keep, inv, 0.0)
+    half = field * inv * half_gain
+    inner = half * (1.5957691216057308 + 0.285419265090401 * (half * half))
+    return half + half * jnp.tanh(inner)
 
 
 def map_kernel(
     left_ref,
     right_ref,
+    trunk_ref,
     gain_ref,
     kern_ref,
     bias_ref,
     weight_ref,
     out_ref,
+    trunk_out_ref,
     lf,
     rf,
+    lp,
+    rp,
     act0,
     field1,
     act1,
+    taps_w,
+    plain,
+    sems,
 ):
     seq = lax.axis_index("seq")
     band = lax.axis_index("band")
     length = SEQ * BINS
+    copies = [pltpu.make_async_copy(trunk_ref, trunk_out_ref, sems.at[12])]
+    for layer in range(2):
+        for p in range(3):
+            for second in range(2):
+                copies.append(
+                    pltpu.make_async_copy(
+                        kern_ref.at[layer, p],
+                        taps_w.at[layer, pl.ds(4 * p + second, 3), :, pl.ds(128 * second, 128)],
+                        sems.at[layer * 6 + p * 2 + second],
+                    )
+                )
+    for copy in copies:
+        copy.start()
+    for layer in range(2):
+        for p in range(3):
+            taps_w[layer, 4 * p + 3, :, 0:128] = jnp.zeros((128, 128), BF16)
+            taps_w[layer, 4 * p, :, 128:256] = jnp.zeros((128, 128), BF16)
     lf[...] = left_ref[...].astype(F32)
-    rf[...] = right_ref[...].astype(F32)
-    place = lax.broadcasted_iota(jnp.int32, (ROWS, 128), 0)
+    rf[0:192] = right_ref[...].astype(F32)
+    for a in range(CHUNK):
+        lp[a] = lf[pl.ds(LEAD + a, LANES, stride=CHUNK)]
+    for t in range(WIDE0 + CHUNK - 1):
+        rp[t] = rf[pl.ds(t + 2, LANES, stride=CHUNK)]
+
+    shape = (CHUNK, LANES, 128)
     first = seq * BINS - LEAD
-
-    def bounds(diag):
+    spot = (
+        lax.broadcasted_iota(jnp.int32, shape, 0)
+        + lax.broadcasted_iota(jnp.int32, shape, 1) * CHUNK
+        + first
+    )
+
+    def inside(diag):
         known = (diag >= 0) & (diag < BANDS * DIAG)
-        low = -first
-        high = jnp.minimum(length, length - diag) - first
-        return low, jnp.where(known, high, low)
-
-    def masked(value, diag):
-        low, high = bounds(diag)
-        return jnp.where((place >= low) & (place < high), value, 0.0)
+        high = jnp.where(known, jnp.minimum(length, length - diag), 0)
+        return (spot >= 0) & (spot < high)
 
     def start_field(delta):
-        value = lf[LEAD : LEAD + ROWS] * rf[pl.ds(delta + 2, ROWS)]
-        return masked(value, band * DIAG + delta - 6).astype(BF16).astype(F32)
-
-    gain0 = gain_ref[0:1]
-    gain1 = gain_ref[1:2]
-
-    @pl.loop(0, WIDE0)
-    def _(delta):
-        act = gelu_norm(start_field(delta), gain0)
-        act0[0, delta] = pltpu.roll(act, 1, 0).astype(BF16)
-        act0[1, delta] = act.astype(BF16)
-        act0[2, delta] = pltpu.roll(act, ROWS - 1, 0).astype(BF16)
-
-    @pl.loop(0, WIDE1 // GROUP)
-    def _(step):
-        diag = step * GROUP
+        return lp[...] * rp[pl.ds(delta, CHUNK)]
+
+    root = float(HEAD) ** 0.5 * 0.5
+    gain0 = gain_ref[0:1].reshape(1, 1, 128) * root
+    gain1 = gain_ref[1:2].reshape(1, 1, 128) * root
+    bias0 = bias_ref[0:1].reshape(1, 1, 128)
+    bias1 = bias_ref[1:2].reshape(1, 1, 128)
+    weight = weight_ref[...].reshape(1, 1, 128)
+
+    def put(dst, where, act, reach):
+        dst[where, pl.ds(reach, CHUNK)] = act.astype(BF16)
+        before = pltpu.roll(act[CHUNK - reach :], 1, 1)
+        after = pltpu.roll(act[:reach], LANES - 1, 1)
+        dst[where, pl.ds(0, reach)] = before.astype(BF16)
+        dst[where, pl.ds(reach + CHUNK, reach)] = after.astype(BF16)
+
+    def first_act(delta):
+        keep = inside(band * DIAG + delta - 6)
+        put(act0, delta, norm_gelu(start_field(delta), gain0, keep), 1)
+
+    def conv(src, layer, slabs, reach):
         taps = jnp.concatenate(
             [
-                act0[p, pl.ds(diag + 2 + q - p, GROUP)].reshape(GROUP * ROWS, 128)
+                jnp.concatenate(
+                    [
+                        src[slab + reach * (j - p), pl.ds(reach * p, CHUNK)].reshape(ROWS, 128)
+                        for slab in slabs
+                    ],
+                    axis=0,
+                )
                 for p in range(3)
-                for q in range(3)
+                for j in range(4)
             ],
             axis=1,
         )
-        term = jnp.dot(taps, kern_ref[0], preferred_element_type=F32)
+        return jnp.dot(
+            taps, taps_w[layer].reshape(12 * 128, 256), preferred_element_type=F32
+        )
+
+    def second_act(step, term):
+        diag = step * GROUP
         for g in range(GROUP):
-            value = term[g * ROWS : (g + 1) * ROWS] + start_field(diag + g + 2) + bias_ref[0:1]
-            value = masked(value, band * DIAG + diag + g - 4).astype(BF16)
-            field1[diag + g] = value
-            act = gelu_norm(value.astype(F32), gain1)
-            act1[0, diag + g] = pltpu.roll(act, 2, 0)[LEAD : LEAD + BINS].astype(BF16)
-            act1[1, diag + g] = act[LEAD : LEAD + BINS].astype(BF16)
-            act1[2, diag + g] = pltpu.roll(act, ROWS - 2, 0)[LEAD : LEAD + BINS].astype(BF16)
-
-    lane = lax.broadcasted_iota(jnp.int32, (BINS, 128), 1)
-    spot = lax.broadcasted_iota(jnp.int32, (BINS, 128), 0) + seq * BINS
-
-    def last(step, found):
+            pair, half = g // 2, g % 2
+            block = term[pair * ROWS : (pair + 1) * ROWS, half * 128 : (half + 1) * 128]
+            value = block.reshape(shape) + start_field(diag + g + 2) + bias0
+            field1[diag + g] = value.astype(BF16)
+            keep = inside(band * DIAG + diag + g - 4)
+            put(act1, diag + g, norm_gelu(value, gain1, keep), 2)
+
+    @pl.loop(0, 2)
+    def _(step):
+        for g in range(GROUP):
+            first_act(step * GROUP + g)
+
+    for copy in copies:
+        copy.wait()
+
+    def conv0(step):
+        slab = step * GROUP + 2
+        return conv(act0, 0, [slab, slab + 2], 1)
+
+    def grow(step, term):
+        fresh = conv0(step)
+        second_act(step - 1, term)
+        for g in range(GROUP):
+            first_act(step * GROUP + 8 + g)
+        return fresh
+
+    steps = WIDE1 // GROUP
+    term = conv0(0)
+    for g in range(GROUP):
+        first_act(8 + g)
+    term = lax.fori_loop(1, steps - 1, grow, term)
+    fresh = conv0(steps - 1)
+    second_act(steps - 2, term)
+    second_act(steps - 1, fresh)
+
+    lane = lax.broadcasted_iota(jnp.int32, shape, 2)
+
+    def conv1(step):
+        slab = step * GROUP + 4
+        return conv(act1, 1, [slab, slab + 1], 2)
+
+    def finish(step, term, found):
         diag = step * GROUP
-        taps = jnp.concatenate(
-            [
-                act1[p, pl.ds(diag + 4 + 2 * (q - p), GROUP)].reshape(GROUP * BINS, 128)
-                for p in range(3)
-                for q in range(3)
-            ],
-            axis=1,
-        )
-        term = jnp.dot(taps, kern_ref[1], preferred_element_type=F32)
         for g in range(GROUP):
-            value = (
-                term[g * BINS : (g + 1) * BINS]
-                + field1[diag + g + 4].astype(F32)[LEAD : LEAD + BINS]
-                + bias_ref[1:2]
-            )
-            value = jnp.where(spot + (band * DIAG + diag + g) < length, value, 0.0)
-            value = value.astype(BF16).astype(F32)
-            contact = jnp.sum(value * weight_ref[...], axis=-1, keepdims=True)
+            pair, half = g % 2, g // 2
+            block = term[pair * ROWS : (pair + 1) * ROWS, half * 128 : (half + 1) * 128]
+            value = block.reshape(shape) + field1[diag + g + 4].astype(F32) + bias1
+            contact = jnp.sum(value * weight, axis=-1, keepdims=True)
             found = jnp.where(lane == diag + g, contact, found)
         return found
 
-    found = lax.fori_loop(0, DIAG // GROUP, last, jnp.zeros((BINS, 128), F32))
-    out_ref[...] = found[:, 0:DIAG]
+    def last(step, carry):
+        term, found = carry
+        fresh = conv1(step)
+        return fresh, finish(step - 1, term, found)
+
+    steps = DIAG // GROUP
+    term, found = lax.fori_loop(1, steps, last, (conv1(0), jnp.zeros(shape, F32)))
+    found = finish(steps - 1, term, found)
+    found = jnp.where(spot + band * DIAG + lane < length, found, 0.0)
+    for a in range(CHUNK):
+        plain[pl.ds(a, LANES, stride=CHUNK)] = found[a]
+    out_ref[...] = plain[LEAD : LEAD + BINS].T[0:DIAG]
 
 
 def local(
@@ -424,19 +505,21 @@
     contact_weight,
 ):
     vmem = pl.BlockSpec(memory_space=pltpu.VMEM)
-    anywhere = pl.BlockSpec(memory_space=pl.ANY)
+    hbm = pl.BlockSpec(memory_space=pltpu.HBM)
     dma = pltpu.SemaphoreType.DMA
-    trunk_out, left, right = pl.pallas_call(
+    trunk, left, right = pl.pallas_call(
         trunk_kernel,
         out_shape=(
             jax.ShapeDtypeStruct((BINS, 128), BF16),
             jax.ShapeDtypeStruct((160, 128), BF16),
             jax.ShapeDtypeStruct((192, 128), BF16),
         ),
-        in_specs=[vmem] * 3 + [anywhere] * 6,
+        in_specs=[hbm] * 9,
         out_specs=(vmem, vmem, vmem),
         scratch_shapes=[
             pltpu.VMEM((BANDS, 128, 128), BF16),
+            pltpu.VMEM((1, 1024), F32),
+            pltpu.VMEM((1, BINS), jnp.int32),
             pltpu.VMEM((1024, 384), BF16),
             pltpu.VMEM((128, 1024), BF16),
             pltpu.VMEM((1024, 256), BF16),
@@ -451,7 +534,7 @@
             pltpu.VMEM((BANDS, 128, 128), BF16),
             pltpu.VMEM((160, 128), BF16),
             pltpu.VMEM((416, 128), BF16),
-            dma((6,)),
+            dma((9,)),
         ]
         + [dma((8,)) for _ in range(18)],
         compiler_params=pltpu.CompilerParams(
@@ -468,28 +551,37 @@
         w_left,
         w_right,
     )
-    contacts = pl.pallas_call(
+    contacts, trunk_out = pl.pallas_call(
         map_kernel,
-        out_shape=jax.ShapeDtypeStruct((BINS, DIAG), F32),
-        in_specs=[vmem] * 6,
-        out_specs=vmem,
+        out_shape=(
+            jax.ShapeDtypeStruct((DIAG, BINS), F32),
+            jax.ShapeDtypeStruct((BINS, 128), BF16),
+        ),
+        in_specs=[vmem, vmem, vmem, vmem, hbm, vmem, vmem],
+        out_specs=(vmem, hbm),
         scratch_shapes=[
             pltpu.VMEM((160, 128), F32),
-            pltpu.VMEM((192, 128), F32),
-            pltpu.VMEM((3, WIDE0, ROWS, 128), BF16),
-            pltpu.VMEM((WIDE1, ROWS, 128), BF16),
-            pltpu.VMEM((3, WIDE1, BINS, 128), BF16),
+            pltpu.VMEM((200, 128), F32),
+            pltpu.VMEM((CHUNK, LANES, 128), F32),
+            pltpu.VMEM((WIDE0 + CHUNK - 1, LANES, 128), F32),
+            pltpu.VMEM((WIDE0, CHUNK + 2, LANES, 128), BF16),
+            pltpu.VMEM((WIDE1, CHUNK, LANES, 128), BF16),
+            pltpu.VMEM((WIDE1, CHUNK + 4, LANES, 128), BF16),
+            pltpu.VMEM((2, 12, 128, 256), BF16),
+            pltpu.VMEM((ROWS, 128), F32),
+            dma((13,)),
         ],
-        compiler_params=pltpu.CompilerParams(vmem_limit_bytes=40 * 1024 * 1024),
+        compiler_params=pltpu.CompilerParams(vmem_limit_bytes=32 * 1024 * 1024),
     )(
         left,
         right,
+        trunk,
         conv_gain,
-        conv_kernel.reshape(2, 9 * 128, 128),
+        conv_kernel,
         conv_bias,
         contact_weight.reshape(1, 128),
     )
-    return (trunk_out, contacts)
+    return (trunk_out, contacts.T)
 
 
 def solution(mesh):

time: 76.4 us -> 66.9 us (0.88)
  Pallas kernels: 66.2 us -> 58 us
  local copies, waits for them, and re-layouts: 9.08 us -> 7.78 us
    pallas_call x1, Pallas kernels: 18.8 us -> 10.5 us  [local(): pl.pallas_call(map_kernel, out_shape=(jax.ShapeDtypeStruct((DIAG, BINS),...]
    unnamed x28 -> x26, local copies, waits for them, and re-layouts: 9.08 us -> 7.78 us
where the time goes in v2:
time: 66.9 us; the launch traced here: 66.5 us
  Pallas kernels  58 us (87%)
  local copies, waits for them, and re-layouts  7.78 us (12%)
  between operations  0.7 us (1%)
    pallas_call x1, Pallas kernels, local(): pl.pallas_call(trunk_kernel, out_shape=(jax.ShapeDtypeStruct((BINS, 128),...  47.5 us
    pallas_call x1, Pallas kernels, local(): pl.pallas_call(map_kernel, out_shape=(jax.ShapeDtypeStruct((DIAG, BINS),...  10.5 us
    unnamed x26, local copies, waits for them, and re-layouts  7.78 us

profile of v2, /device:TPU:1, one launch (start us, length us, event | category | flops | bytes accessed | tf_op | source)
XLA Modules:
  0.0 66.5 jit_solution(726030658066921972)
XLA Ops:
  0.6 0.0 copy-start.8
  0.6 0.0 copy-start.11
  0.7 0.7 %copy-done.8 = f32[1024]{0:T(1024)S(1)} copy-done((f32[1024]{0:T(1024)S(1)}, f32[1024]{0:T(1024)}, u32[]{:S(2)}) %copy-start.8) | copy-done | bytes 4120
  1.3 0.0 copy-done.11
  1.3 0.0 copy-start.1
  1.3 0.9 %copy-done.1 = bf16[1024,128]{1,0:T(8,128)(2,1)S(1)} copy-done((bf16[1024,128]{1,0:T(8,128)(2,1)S(1)}, bf16[1024,128]{1,0:T(8,128)(2,1)}, u32[]{:S(2)}) %copy-start.1) | copy-done | bytes 262168
  2.3 0.0 copy-start.2
  2.3 0.9 %copy-done.2 = bf16[1024,128]{1,0:T(8,128)(2,1)S(1)} copy-done((bf16[1024,128]{1,0:T(8,128)(2,1)S(1)}, bf16[1024,128]{1,0:T(8,128)(2,1)}, u32[]{:S(2)}) %copy-start.2) | copy-done | bytes 262168
  3.2 0.0 copy-start.3
  3.2 0.9 %copy-done.3 = bf16[1024,128]{1,0:T(8,128)(2,1)S(1)} copy-done((bf16[1024,128]{1,0:T(8,128)(2,1)S(1)}, bf16[1024,128]{1,0:T(8,128)(2,1)}, u32[]{:S(2)}) %copy-start.3) | copy-done | bytes 262168
  4.2 0.0 copy-start.4
  4.2 0.9 %copy-done.4 = bf16[128,1024]{1,0:T(8,128)(2,1)S(1)} copy-done((bf16[128,1024]{1,0:T(8,128)(2,1)S(1)}, bf16[128,1024]{1,0:T(8,128)(2,1)}, u32[]{:S(2)}) %copy-start.4) | copy-done | bytes 262168
  5.1 0.0 copy-start.5
  5.1 0.9 %copy-done.5 = bf16[1024,128]{1,0:T(8,128)(2,1)S(1)} copy-done((bf16[1024,128]{1,0:T(8,128)(2,1)S(1)}, bf16[1024,128]{1,0:T(8,128)(2,1)}, u32[]{:S(2)}) %copy-start.5) | copy-done | bytes 262168
  6.1 0.0 copy-start.6
  6.1 0.9 %copy-done.6 = bf16[1024,128]{1,0:T(8,128)(2,1)S(1)} copy-done((bf16[1024,128]{1,0:T(8,128)(2,1)S(1)}, bf16[1024,128]{1,0:T(8,128)(2,1)}, u32[]{:S(2)}) %copy-start.6) | copy-done | bytes 262168
  7.0 0.0 copy-start.7
  7.0 0.8 %copy-done.7 = bf16[128,128]{1,0:T(8,128)(2,1)S(1)} copy-done((bf16[128,128]{1,0:T(8,128)(2,1)S(1)}, bf16[128,128]{1,0:T(8,128)(2,1)}, u32[]{:S(2)}) %copy-start.7) | copy-done | bytes 32792
  7.8 0.0 copy-start
  7.8 0.0 copy-start.10
  7.8 47.5 %shard_map.140 = (bf16[128,128]{1,0:T(8,128)(2,1)S(1)}, bf16[160,128]{1,0:T(8,128)(2,1)S(1)}, bf16[192,128]{1,0:T(8,128)(2,1)S(1)}) custom-call(bf16[128,128]{1,0:T(8,128)(2,1)S(1)} %copy-done.7, s32[1,128]{1,0:T(1,128)S(1)} %bitcast.5, f32[1,1024]{1,0:T(1,128)S(1)} %bitcast.4, bf16[1024,128]{1,0:T(8,128)(2,1)S(1)} %copy-done.1, ...), custom_call_target="tpu_custom_call" | custom-call | tf_op jit(solution)/shard_map/pallas_call | solution.py:510
  55.3 0.0 copy-start.9
  55.3 0.0 copy-start.12
  55.3 0.0 copy-done
  55.4 0.0 copy-done.10
  55.4 0.6 copy-done.9
  56.0 0.0 copy-done.12
  56.0 10.5 %shard_map.141 = (f32[32,128]{1,0:T(8,128)}, bf16[128,128]{1,0:T(8,128)(2,1)}) custom-call(bf16[160,128]{1,0:T(8,128)(2,1)S(1)} %get-tuple-element.7.left_ref, bf16[192,128]{1,0:T(8,128)(2,1)S(1)} %get-tuple-element.8.right_ref, bf16[128,128]{1,0:T(8,128)(2,1)S(1)} %get-tuple-element.9.trunk_ref, f32[2,128]{1,0:T(2,128)S(1)} %copy-done.9, ...), custom_call_target="tpu_custom_call" | custom-call | tf_op jit(solution)/shard_map/pallas_call | solution.py:554
Async XLA Ops:
  0.6 0.7 %copy-start.8 = (f32[1024]{0:T(1024)S(1)}, f32[1024]{0:T(1024)}, u32[]{:S(2)}) copy-start(f32[1024]{0:T(1024)} %param.15) | copy-start | bytes 12292
  0.6 0.7 %copy-start.11 = (s32[128]{0:T(128)S(1)}, s32[128]{0:T(128)}, u32[]{:S(2)}) copy-start(s32[128]{0:T(128)} %param.14) | copy-start | bytes 1540
  1.3 1.0 %copy-start.1 = (bf16[1024,128]{1,0:T(8,128)(2,1)S(1)}, bf16[1024,128]{1,0:T(8,128)(2,1)}, u32[]{:S(2)}) copy-start(bf16[1024,128]{1,0:T(8,128)(2,1)} %wq_ref.1) | copy-start | bytes 786436
  2.3 0.9 %copy-start.2 = (bf16[1024,128]{1,0:T(8,128)(2,1)S(1)}, bf16[1024,128]{1,0:T(8,128)(2,1)}, u32[]{:S(2)}) copy-start(bf16[1024,128]{1,0:T(8,128)(2,1)} %wk_ref.1) | copy-start | bytes 786436
  3.2 0.9 %copy-start.3 = (bf16[1024,128]{1,0:T(8,128)(2,1)S(1)}, bf16[1024,128]{1,0:T(8,128)(2,1)}, u32[]{:S(2)}) copy-start(bf16[1024,128]{1,0:T(8,128)(2,1)} %wv_ref.1) | copy-start | bytes 786436
  4.2 0.9 %copy-start.4 = (bf16[128,1024]{1,0:T(8,128)(2,1)S(1)}, bf16[128,1024]{1,0:T(8,128)(2,1)}, u32[]{:S(2)}) copy-start(bf16[128,1024]{1,0:T(8,128)(2,1)} %wout_ref.1) | copy-start | bytes 786436
  5.1 0.9 %copy-start.5 = (bf16[1024,128]{1,0:T(8,128)(2,1)S(1)}, bf16[1024,128]{1,0:T(8,128)(2,1)}, u32[]{:S(2)}) copy-start(bf16[1024,128]{1,0:T(8,128)(2,1)} %wl_ref.1) | copy-start | bytes 786436
  6.1 0.9 %copy-start.6 = (bf16[1024,128]{1,0:T(8,128)(2,1)S(1)}, bf16[1024,128]{1,0:T(8,128)(2,1)}, u32[]{:S(2)}) copy-start(bf16[1024,128]{1,0:T(8,128)(2,1)} %wr_ref.1) | copy-start | bytes 786436
  7.0 0.8 %copy-start.7 = (bf16[128,128]{1,0:T(8,128)(2,1)S(1)}, bf16[128,128]{1,0:T(8,128)(2,1)}, u32[]{:S(2)}) copy-start(bf16[128,128]{1,0:T(8,128)(2,1)} %tok_ref.1) | copy-start | bytes 98308
  7.8 47.6 %copy-start = (bf16[2,3,3,128,128]{4,3,2,1,0:T(8,128)(2,1)S(1)}, bf16[2,3,3,128,128]{4,3,2,1,0:T(8,128)(2,1)}, u32[]{:S(2)}) copy-start(bf16[2,3,3,128,128]{4,3,2,1,0:T(8,128)(2,1)} %kern_ref.1) | copy-start | bytes 1769476
  7.8 47.6 %copy-start.10 = (f32[2,128]{1,0:T(2,128)S(1)}, f32[2,128]{1,0:T(2,128)}, u32[]{:S(2)}) copy-start(f32[2,128]{1,0:T(2,128)} %bias_ref.1) | copy-start | bytes 3076
  55.3 0.7 %copy-start.9 = (f32[2,128]{1,0:T(2,128)S(1)}, f32[2,128]{1,0:T(2,128)}, u32[]{:S(2)}) copy-start(f32[2,128]{1,0:T(2,128)} %gain_ref.1) | copy-start | bytes 3076
  55.3 0.7 %copy-start.12 = (f32[128]{0:T(128)S(1)}, f32[128]{0:T(128)}, u32[]{:S(2)}) copy-start(f32[128]{0:T(128)} %param.25) | copy-start | bytes 1540

commit v3 on v1

v3 whole, which is shorter than its diff:
```python
import jax
import jax.numpy as jnp
from jax import lax
from jax.experimental import pallas as pl
from jax.experimental.pallas import tpu as pltpu
from jax.sharding import PartitionSpec as P

HEAD = 128
DIAG = 32
BINS = 128
EPS = 1e-06
BANDS = 8
RING = 8
SEQ = 32
MESH = pl.DeviceIdType.MESH
F32 = jnp.float32
BF16 = jnp.bfloat16


def remote(src, dst, send_sem, recv_sem, **device):
    return pltpu.make_async_remote_copy(
        src_ref=src,
        dst_ref=dst,
        send_sem=send_sem,
        recv_sem=recv_sem,
        device_id=device,
        device_id_type=MESH,
    )


CHUNK = 9
LANES = 16
ROWS = CHUNK * LANES
LEAD = 8
WIDE0 = 44
WIDE1 = 40
GROUP = 4


def norm_gelu(field, half_gain, keep):
    squares = jnp.sum(field * field, axis=-1, keepdims=True)
    inv = lax.rsqrt(squares + HEAD * EPS)
    if keep is not None:
        inv = jnp.where(keep, inv, 0.0)
    half = field * inv * half_gain
    inner = half * (1.5957691216057308 + 0.285419265090401 * (half * half))
    return half + half * jnp.tanh(inner)


def pair_map(
    seq,
    band,
    leftbuf,
    rightbuf,
    gain_ref,
    bias_ref,
    weight_ref,
    out_ref,
    lf,
    rf,
    lp,
    rp,
    act0,
    field1,
    act1,
    taps_w,
    plain,
    loads,
):
    length = SEQ * BINS
    lf[...] = leftbuf[...].astype(F32)
    rf[0:192] = rightbuf[pl.ds(pl.multiple_of(band * DIAG, DIAG), 192)].astype(F32)
    for a in range(CHUNK):
        lp[a] = lf[pl.ds(LEAD + a, LANES, stride=CHUNK)]
    for t in range(WIDE0 + CHUNK - 1):
        rp[t] = rf[pl.ds(t + 2, LANES, stride=CHUNK)]

    shape = (CHUNK, LANES, 128)
    first = seq * BINS - LEAD
    spot = (
        lax.broadcasted_iota(jnp.int32, shape, 0)
        + lax.broadcasted_iota(jnp.int32, shape, 1) * CHUNK
        + first
    )

    def inside(diag):
        known = (diag >= 0) & (diag < BANDS * DIAG)
        high = jnp.where(known, jnp.minimum(length, length - diag), 0)
        return (spot >= 0) & (spot < high)

    def start_field(delta):
        return lp[...] * rp[pl.ds(delta, CHUNK)]

    root = float(HEAD) ** 0.5 * 0.5
    gain0 = gain_ref[0:1].reshape(1, 1, 128) * root
    gain1 = gain_ref[1:2].reshape(1, 1, 128) * root
    bias0 = bias_ref[0:1].reshape(1, 1, 128)
    bias1 = bias_ref[1:2].reshape(1, 1, 128)
    weight = weight_ref[...].reshape(1, 1, 128)

    def put(dst, where, act, reach):
        dst[where, pl.ds(reach, CHUNK)] = act.astype(BF16)
        before = pltpu.roll(act[CHUNK - reach :], 1, 1)
        after = pltpu.roll(act[:reach], LANES - 1, 1)
        dst[where, pl.ds(0, reach)] = before.astype(BF16)
        dst[where, pl.ds(reach + CHUNK, reach)] = after.astype(BF16)

    def first_act(delta):
        keep = inside(band * DIAG + delta - 6)
        put(act0, delta, norm_gelu(start_field(delta), gain0, keep), 1)

    def conv(src, layer, slabs, reach):
        taps = jnp.concatenate(
            [
                jnp.concatenate(
                    [
                        src[slab + reach * (j - p), pl.ds(reach * p, CHUNK)].reshape(ROWS, 128)
                        for slab in slabs
                    ],
                    axis=0,
                )
                for p in range(3)
                for j in range(4)
            ],
            axis=1,
        )
        return jnp.dot(
            taps, taps_w[layer].reshape(12 * 128, 256), preferred_element_type=F32
        )

    def second_act(step, term):
        diag = step * GROUP
        for g in range(GROUP):
            pair, half = g // 2, g % 2
            block = term[pair * ROWS : (pair + 1) * ROWS, half * 128 : (half + 1) * 128]
            value = block.reshape(shape) + start_field(diag + g + 2) + bias0
            field1[diag + g] = value.astype(BF16)
            keep = inside(band * DIAG + diag + g - 4)
            put(act1, diag + g, norm_gelu(value, gain1, keep), 2)

    @pl.loop(0, 2)
    def _(step):
        for g in range(GROUP):
            first_act(step * GROUP + g)

    for load in loads:
        load.wait()

    def conv0(step):
        slab = step * GROUP + 2
        return conv(act0, 0, [slab, slab + 2], 1)

    def grow(step, term):
        fresh = conv0(step)
        second_act(step - 1, term)
        for g in range(GROUP):
            first_act(step * GROUP + 8 + g)
        return fresh

    steps = WIDE1 // GROUP
    term = conv0(0)
    for g in range(GROUP):
        first_act(8 + g)
    term = lax.fori_loop(1, steps - 1, grow, term)
    fresh = conv0(steps - 1)
    second_act(steps - 2, term)
    second_act(steps - 1, fresh)

    lane = lax.broadcasted_iota(jnp.int32, shape, 2)

    def conv1(step):
        slab = step * GROUP + 4
        return conv(act1, 1, [slab, slab + 1], 2)

    def finish(step, term, found):
        diag = step * GROUP
        for g in range(GROUP):
            pair, half = g % 2, g // 2
            block = term[pair * ROWS : (pair + 1) * ROWS, half * 128 : (half + 1) * 128]
            value = block.reshape(shape) + field1[diag + g + 4].astype(F32) + bias1
            contact = jnp.sum(value * weight, axis=-1, keepdims=True)
            found = jnp.where(lane == diag + g, contact, found)
        return found

    def last(step, carry):
        term, found = carry
        fresh = conv1(step)
        return fresh, finish(step - 1, term, found)

    steps = DIAG // GROUP
    term, found = lax.fori_loop(1, steps, last, (conv1(0), jnp.zeros(shape, F32)))
    found = finish(steps - 1, term, found)
    found = jnp.where(spot + band * DIAG + lane < length, found, 0.0)
    for a in range(CHUNK):
        plain[pl.ds(a, LANES, stride=CHUNK)] = found[a]
    out_ref[...] = plain[LEAD : LEAD + BINS].T[0:DIAG]


def trunk_kernel(
    tok_ref,
    map_ref,
    gain_ref,
    wq_ref,
    wk_ref,
    wv_ref,
    wout_ref,
    wl_ref,
    wr_ref,
    cgain_ref,
    kern_ref,
    bias_ref,
    weight_ref,
    trunk_ref,
    out_ref,
    tok_all,
    gain_v,
    map_v,
    wqkv,
    wout,
    wlr,
    m_all,
    wcol_all,
    q_all,
    kv,
    o_send,
    o_recv,
    st_send,
    st_recv,
    att_all,
    leftbuf,
    rightbuf,
    cgain_v,
    bias_v,
    weight_v,
    lf,
    rf,
    lp,
    rp,
    act0,
    field1,
    act1,
    taps_w,
    plain,
    local_sem,
    tap_sem,
    tok_s,
    tok_r,
    m_s,
    m_r,
    wc_s,
    wc_r,
    q_s,
    q_r,
    kv_s,
    kv_r,
    o_s,
    o_r,
    st_s,
    st_r,
    att_s,
    att_r,
    edge_s,
    edge_r,
):
    seq = lax.axis_index("seq")
    band = lax.axis_index("band")
    core = seq % 2
    ring = (seq // 2) % RING
    half = seq // (2 * RING)
    row = band // 2
    side = band % 2

    def seq_of(half_, ring_, core_):
        return half_ * (2 * RING) + ring_ * 2 + core_

    along = {k: seq_of(half, (ring + RING + k) % RING, core) for k in (-2, -1, 1, 2)}
    mates = [
        None,
        seq_of(half, ring, 1 - core),
        seq_of(1 - half, ring, core),
        seq_of(1 - half, ring, 1 - core),
    ]
    near = {k: (seq + SEQ + k) % SEQ for k in (-3, -2, -1, 1, 2, 3)}

    def to_band(k):
        return (band + k) % BANDS

    def from_band(k):
        return (band + BANDS - k) % BANDS

    loads = [
        pltpu.make_async_copy(tok_ref, tok_all.at[band], local_sem.at[0]),
        pltpu.make_async_copy(gain_ref, gain_v, local_sem.at[1]),
        pltpu.make_async_copy(map_ref, map_v, local_sem.at[2]),
        pltpu.make_async_copy(wout_ref, wout, local_sem.at[3]),
        pltpu.make_async_copy(wl_ref, wlr.at[:, pl.ds(0, 128)], local_sem.at[4]),
        pltpu.make_async_copy(wr_ref, wlr.at[:, pl.ds(128, 128)], local_sem.at[5]),
        pltpu.make_async_copy(wq_ref, wqkv.at[:, pl.ds(0, 128)], local_sem.at[6]),
        pltpu.make_async_copy(wk_ref, wqkv.at[:, pl.ds(128, 128)], local_sem.at[7]),
        pltpu.make_async_copy(wv_ref, wqkv.at[:, pl.ds(256, 128)], local_sem.at[8]),
        pltpu.make_async_copy(cgain_ref, cgain_v, local_sem.at[9]),
        pltpu.make_async_copy(bias_ref, bias_v, local_sem.at[10]),
        pltpu.make_async_copy(weight_ref, weight_v, local_sem.at[11]),
    ]
    tap_loads = [
        pltpu.make_async_copy(
            kern_ref.at[layer, p],
            taps_w.at[layer, pl.ds(4 * p + second, 3), :, pl.ds(128 * second, 128)],
            tap_sem.at[layer * 6 + p * 2 + second],
        )
        for layer in range(2)
        for p in range(3)
        for second in range(2)
    ]
    for load in loads:
        load.start()

    barrier = pltpu.get_barrier_semaphore()
    others = [{"seq": other} for other in list(near.values()) + list(along.values()) + mates[1:]]
    others += [{"band": to_band(k)} for k in range(1, BANDS)]
    for other in others:
        pl.semaphore_signal(barrier, inc=1, device_id=other, device_id_type=MESH)
    for load in tap_loads:
        load.start()
    for layer in range(2):
        for p in range(3):
            taps_w[layer, 4 * p + 3, :, 0:128] = jnp.zeros((128, 128), BF16)
            taps_w[layer, 4 * p, :, 128:256] = jnp.zeros((128, 128), BF16)
    pl.semaphore_wait(barrier, len(others))

    def band_send(src, dst_all, s_sem, r_sem, k):
        return remote(src, dst_all.at[band], s_sem.at[k], r_sem.at[k], band=to_band(k))

    def band_recv(dst_all, s_sem, r_sem, k):
        slot = dst_all.at[from_band(k)]
        return remote(slot, slot, s_sem.at[k], r_sem.at[k], band=to_band(k))

    tok_sends = [band_send(tok_ref, tok_all, tok_s, tok_r, k) for k in range(1, BANDS)]
    for send in tok_sends:
        send.start()

    for load in loads:
        load.wait()
    m_all[band] = jnp.dot(wout[...], wlr[...], preferred_element_type=F32).astype(BF16)
    offset = ((map_v[...] - 1).astype(F32) * 1000000000.0).astype(BF16)
    kv[0, 128:144] = jnp.broadcast_to(offset, (16, 128))
    for k in range(1, BANDS):
        band_recv(tok_all, tok_s, tok_r, k).wait_recv()

    floats = jnp.concatenate([tok_all[c] for c in range(BANDS)], axis=1).astype(F32)
    inv = lax.rsqrt(jnp.mean(floats * floats, axis=-1, keepdims=True) + EPS)
    normed = (floats * inv * gain_v[...]).astype(BF16)
    qkv = jnp.dot(normed, wqkv[...], preferred_element_type=F32)
    kv[0, 0:128] = qkv[:, 128:256].astype(BF16)
    kv[0, 144:272] = qkv[:, 256:384].T.astype(BF16)
    q_all[0] = qkv[:, 0:128].astype(BF16)

    def kv_copy(src, dst, sem, hops, rows=None):
        where, landed = kv.at[src], kv.at[dst]
        arrival = dst
        if rows is not None:
            where, landed = where.at[pl.ds(*rows)], landed.at[pl.ds(*rows)]
            arrival = dst if rows[0] == 0 else 0
        return remote(where, landed, kv_s.at[sem], kv_r.at[arrival], seq=along[hops])

    upper, lower = (0, 144), (144, 128)
    one = kv_copy(0, 1, 0, 1)
    seven = kv_copy(0, 7, 1, -1)
    two = kv_copy(0, 2, 2, 2)
    six = kv_copy(0, 6, 3, -2)
    three = kv_copy(1, 3, 4, 2)
    five = kv_copy(7, 5, 5, -2)
    four_up = kv_copy(2, 4, 6, 2, upper)
    four_low = kv_copy(6, 4, 7, -2, lower)
    q_copies = [
        remote(q_all.at[0], q_all.at[k], q_s.at[k], q_r.at[k], seq=mates[k]) for k in (1, 2, 3)
    ]
    for copy in [one, seven] + q_copies + [two, six]:
        copy.start()

    across = row * 2 + 1 - side

    def row_peer(k, side_):
        return ((row + 4 + k) % 4) * 2 + side_

    m_own = [remote(m_all.at[band], m_all.at[band], m_s.at[0], m_r.at[0], band=across)] + [
        remote(m_all.at[band], m_all.at[band], m_s.at[k], m_r.at[k], band=row_peer(k, side))
        for k in (1, 2, 3)
    ]
    m_relay = [
        remote(
            m_all.at[across], m_all.at[across], m_s.at[3 + k], m_r.at[3 + k], band=row_peer(k, side)
        )
        for k in (1, 2, 3)
    ]
    m_arrivals = [
        remote(m_all.at[slot], m_all.at[slot], m_s.at[sem], m_r.at[sem], band=across)
        for slot, sem in [(across, 0)]
        + [(row_peer(-k, side), k) for k in (1, 2, 3)]
        + [(row_peer(-k, 1 - side), 3 + k) for k in (1, 2, 3)]
    ]
    for send in m_own:
        send.start()
    keep = jnp.broadcast_to(map_v[...].astype(F32), (128, 128)).T
    keep = jnp.concatenate([keep, keep], axis=1)
    lr_tok = jnp.dot(floats.astype(BF16), wlr[...], preferred_element_type=F32)
    for copy in q_copies:
        copy.wait_recv()
    queries = jnp.concatenate([q_all[k] for k in range(4)], axis=0)

    def attend(state, slots):
        keys = jnp.concatenate([kv[j, 0:128] for j in slots], axis=0)
        values_t = jnp.concatenate([kv[j, 144:272] for j in slots], axis=1)
        offs = jnp.concatenate(
            [jnp.broadcast_to(kv[j, 128:144][0:1].astype(F32), (128, 128)).T for j in slots],
            axis=0,
        )
        offs = jnp.concatenate([offs] * 4, axis=1)
        scores = (
            lax.dot_general(
                keys, queries, (((1,), (1,)), ((), ())), preferred_element_type=F32
            )
            * HEAD ** (-0.5)
            + offs
        )
        block_top = jnp.max(scores, axis=0, keepdims=True)
        if state is None:
            top = block_top
        else:
            top = jnp.maximum(state[0], block_top)
        weights = jnp.exp(scores - top)
        block_sum = jnp.sum(weights, axis=0, keepdims=True)
        mixed = jnp.dot(values_t, weights.astype(BF16), preferred_element_type=F32)
        if state is None:
            return top, block_sum, mixed
        fade = jnp.exp(state[0] - top)
        return top, state[1] * fade + block_sum, state[2] * fade + mixed

    state = attend(None, [0])
    one.wait_recv()
    three.start()
    seven.wait_recv()
    five.start()
    state = attend(state, [1, 7])
    m_arrivals[0].wait_recv()
    for send in m_relay:
        send.start()
    two.wait_recv()
    four_up.start()
    six.wait_recv()
    four_low.start()
    state = attend(state, [2, 6])
    three.wait_recv()
    five.wait_recv()
    state = attend(state, [3, 5])
    four_up.wait_recv()
    four_low.wait_recv()
    top, total, mixed = attend(state, [4])

    mixed = mixed / total
    o_copies = []
    for k in (1, 2, 3):
        lanes = slice(k * 128, (k + 1) * 128)
        o_send[k] = mixed[:, lanes].astype(BF16)
        st_send[k, 0:4] = jnp.broadcast_to(top[:, lanes], (4, 128))
        st_send[k, 4:8] = jnp.broadcast_to(total[:, lanes], (4, 128))
        o_copies.append(
            remote(st_send.at[k], st_recv.at[k], st_s.at[k], st_r.at[k], seq=mates[k])
        )
        o_copies.append(remote(o_send.at[k], o_recv.at[k], o_s.at[k], o_r.at[k], seq=mates[k]))
    for copy in o_copies:
        copy.start()
    for copy in o_copies:
        copy.wait_recv()
    tops = [top[:, 0:128]] + [st_recv[k, 0:1] for k in (1, 2, 3)]
    sums = [total[:, 0:128]] + [st_recv[k, 4:5] for k in (1, 2, 3)]
    parts = [mixed[:, 0:128]] + [o_recv[k].astype(F32) for k in (1, 2, 3)]
    best = jnp.maximum(jnp.maximum(tops[0], tops[1]), jnp.maximum(tops[2], tops[3]))
    shares = [s * jnp.exp(t - best) for s, t in zip(sums, tops)]
    share_sum = shares[0] + shares[1] + shares[2] + shares[3]
    attended = (
        parts[0] * shares[0] + parts[1] * shares[1] + parts[2] * shares[2] + parts[3] * shares[3]
    ) / share_sum
    att_all[band] = attended.T.astype(BF16)
    att_sends = [band_send(att_all.at[band], att_all, att_s, att_r, k) for k in range(1, BANDS)]
    for send in att_sends:
        send.start()
    for copy in m_arrivals[1:]:
        copy.wait_recv()
    for k in range(1, BANDS):
        band_recv(att_all, att_s, att_r, k).wait_recv()

    heads = jnp.concatenate([att_all[c] for c in range(BANDS)], axis=1)
    both = lr_tok + jnp.dot(
        heads, m_all[...].reshape(BANDS * 128, 256), preferred_element_type=F32
    )
    both = (both * keep).astype(BF16)
    leftbuf[16:144] = both[:, 0:128]
    rightbuf[16:144] = both[:, 128:256]

    def edge(src, dst, sem, other):
        return remote(src, dst, edge_s.at[sem], edge_r.at[sem], seq=other)

    own = rightbuf.at[pl.ds(16, 128)]
    edges = [
        edge(own, rightbuf.at[pl.ds(272, 128)], 1, near[-2]),
        edge(own, rightbuf.at[pl.ds(144, 128)], 0, near[-1]),
        edge(rightbuf.at[pl.ds(16, 16)], rightbuf.at[pl.ds(400, 16)], 2, near[-3]),
        edge(rightbuf.at[pl.ds(128, 16)], rightbuf.at[pl.ds(0, 16)], 3, near[1]),
        edge(leftbuf.at[pl.ds(16, 16)], leftbuf.at[pl.ds(144, 16)], 4, near[-1]),
        edge(leftbuf.at[pl.ds(128, 16)], leftbuf.at[pl.ds(0, 16)], 5, near[1]),
    ]
    for copy in edges:
        copy.start()
    wc_sends = [
        band_send(
            wout.at[:, pl.ds(pl.multiple_of(to_band(k) * 128, 128), 128)], wcol_all, wc_s, wc_r, k
        )
        for k in range(1, BANDS)
    ]
    for send in wc_sends:
        send.start()
    wcol_all[band] = wout[:, pl.ds(pl.multiple_of(band * 128, 128), 128)]
    for copy in edges:
        copy.wait_recv()
    pair_map(
        seq,
        band,
        leftbuf,
        rightbuf,
        cgain_v,
        bias_v,
        weight_v,
        out_ref,
        lf,
        rf,
        lp,
        rp,
        act0,
        field1,
        act1,
        taps_w,
        plain,
        tap_loads,
    )
    for k in range(1, BANDS):
        band_recv(wcol_all, wc_s, wc_r, k).wait_recv()
    heads = jnp.concatenate([att_all[c] for c in range(BANDS)], axis=1)
    summed = jnp.dot(
        heads, wcol_all[...].reshape(BANDS * 128, 128), preferred_element_type=F32
    )
    trunk_ref[...] = (tok_all[band].astype(F32) + summed).astype(BF16)
    for send in tok_sends + q_copies + m_own + m_relay + o_copies + att_sends + edges + wc_sends:
        send.wait_send()
    for send in [one, two, three, five, six, seven, four_up, four_low]:
        send.wait_send()


def local(
    tokens,
    mappable,
    attn_gain,
    w_query,
    w_key,
    w_value,
    w_out,
    w_left,
    w_right,
    conv_gain,
    conv_kernel,
    conv_bias,
    contact_weight,
):
    vmem = pl.BlockSpec(memory_space=pltpu.VMEM)
    hbm = pl.BlockSpec(memory_space=pltpu.HBM)
    dma = pltpu.SemaphoreType.DMA
    trunk_out, contacts = pl.pallas_call(
        trunk_kernel,
        out_shape=(
            jax.ShapeDtypeStruct((BINS, 128), BF16),
            jax.ShapeDtypeStruct((DIAG, BINS), F32),
        ),
        in_specs=[hbm] * 13,
        out_specs=(vmem, vmem),
        scratch_shapes=[
            pltpu.VMEM((BANDS, 128, 128), BF16),
            pltpu.VMEM((1, 1024), F32),
            pltpu.VMEM((1, BINS), jnp.int32),
            pltpu.VMEM((1024, 384), BF16),
            pltpu.VMEM((128, 1024), BF16),
            pltpu.VMEM((1024, 256), BF16),
            pltpu.VMEM((BANDS, 128, 256), BF16),
            pltpu.VMEM((BANDS, 128, 128), BF16),
            pltpu.VMEM((4, 128, 128), BF16),
            pltpu.VMEM((RING, 272, 128), BF16),
            pltpu.VMEM((4, 128, 128), BF16),
            pltpu.VMEM((4, 128, 128), BF16),
            pltpu.VMEM((4, 8, 128), F32),
            pltpu.VMEM((4, 8, 128), F32),
            pltpu.VMEM((BANDS, 128, 128), BF16),
            pltpu.VMEM((160, 128), BF16),
            pltpu.VMEM((416, 128), BF16),
            pltpu.VMEM((2, 128), F32),
            pltpu.VMEM((2, 128), F32),
            pltpu.VMEM((1, 128), F32),
            pltpu.VMEM((160, 128), F32),
            pltpu.VMEM((200, 128), F32),
            pltpu.VMEM((CHUNK, LANES, 128), F32),
            pltpu.VMEM((WIDE0 + CHUNK - 1, LANES, 128), F32),
            pltpu.VMEM((WIDE0, CHUNK + 2, LANES, 128), BF16),
            pltpu.VMEM((WIDE1, CHUNK, LANES, 128), BF16),
            pltpu.VMEM((WIDE1, CHUNK + 4, LANES, 128), BF16),
            pltpu.VMEM((2, 12, 128, 256), BF16),
            pltpu.VMEM((ROWS, 128), F32),
            dma((12,)),
            dma((12,)),
        ]
        + [dma((8,)) for _ in range(18)],
        compiler_params=pltpu.CompilerParams(
            collective_id=0, has_side_effects=True, vmem_limit_bytes=60 * 1024 * 1024
        ),
    )(
        tokens,
        mappable.reshape(1, BINS),
        attn_gain.reshape(1, -1),
        w_query,
        w_key,
        w_value,
        w_out,
        w_left,
        w_right,
        conv_gain,
        conv_kernel,
        conv_bias,
        contact_weight.reshape(1, 128),
    )
    return (trunk_out, contacts.T)


def solution(mesh):
    return jax.shard_map(
        local,
        mesh=mesh,
        in_specs=(
            P("seq", "band"),
            P("seq"),
            P(),
            P(None, "band"),
            P(None, "band"),
            P(None, "band"),
            P("band", None),
            P(),
            P(),
            P(),
            P(),
            P(),
            P(),
        ),
        out_specs=(P("seq", "band"), P("seq", "band")),
        check_vma=False,
    )
```

time: 76.4 us -> 58.2 us (0.76)
  Pallas kernels: 66.2 us -> 55.4 us
  local copies, waits for them, and re-layouts: 9.08 us -> 1.99 us
    pallas_call x1 -> x0, Pallas kernels: 18.8 us -> none  [local(): pl.pallas_call(map_kernel, out_shape=jax.ShapeDtypeStruct((BINS, DIAG), F...]
    pallas_call x1, Pallas kernels: 47.4 us -> 55.4 us  [local(): pl.pallas_call(trunk_kernel, out_shape=(jax.ShapeDtypeStruct((BINS, 128),...]
    unnamed x28 -> x4, local copies, waits for them, and re-layouts: 9.08 us -> 1.99 us
where the time goes in v3:
time: 58.2 us; the launch traced here: 58 us
  Pallas kernels  55.4 us (95%)
  local copies, waits for them, and re-layouts  1.99 us (3%)
  between operations  0.65 us (1%)
    pallas_call x1, Pallas kernels, local(): pl.pallas_call(trunk_kernel, out_shape=(jax.ShapeDtypeStruct((BINS, 128),...  55.4 us
    unnamed x4, local copies, waits for them, and re-layouts  1.99 us

profile of v3, /device:TPU:1, one launch (start us, length us, event | category | flops | bytes accessed | tf_op | source)
XLA Modules:
  0.0 58.0 jit_solution(8595869008211487686)
XLA Ops:
  0.6 55.4 %shard_map.140 = (bf16[128,128]{1,0:T(8,128)(2,1)}, f32[32,128]{1,0:T(8,128)}) custom-call(bf16[128,128]{1,0:T(8,128)(2,1)} %tok_ref.1, s32[1,128]{1,0:T(1,128)} %bitcast.6, f32[1,1024]{1,0:T(1,128)} %bitcast.5, bf16[1024,128]{1,0:T(8,128)(2,1)} %wq_ref.1, bf16[1024,128]{1,0:T(8,128)(2,1)} %wk_ref.1, bf16[1024,128]{1,0:T(8,128)(2,1)} %wv_ref.1, ...), custom_call_target="tpu_custom_call" | custom-call | tf_op jit(solution)/shard_map/pallas_call | solution.py:577
  56.0 0.0 copy-start
  56.0 1.4 %copy.17 = bf16[128,128]{1,0:T(8,128)(2,1)} copy(bf16[128,128]{1,0:T(8,128)(2,1)} %get-tuple-element.8) | data formatting | bytes 65536
  57.4 0.0 copy-done
  57.4 0.6 %copy.18 = f32[128,32]{0,1:T(8,128)} copy(f32[128,32]{0,1:T(8,128)S(1)} %bitcast.4) | data formatting | bytes 32768
Async XLA Ops:
  56.0 1.4 %copy-start = (f32[32,128]{1,0:T(8,128)S(1)}, f32[32,128]{1,0:T(8,128)}, u32[]{:S(2)}) copy-start(f32[32,128]{1,0:T(8,128)} %get-tuple-element.5) | copy-start | bytes 49156

commit v4 on v3

--- a/solution.py
+++ b/solution.py
@@ -11,6 +11,7 @@
 EPS = 1e-06
 BANDS = 8
 RING = 8
+LINE = 4
 SEQ = 32
 MESH = pl.DeviceIdType.MESH
 F32 = jnp.float32
@@ -273,13 +274,19 @@
     def seq_of(half_, ring_, core_):
         return half_ * (2 * RING) + ring_ * 2 + core_
 
-    along = {k: seq_of(half, (ring + RING + k) % RING, core) for k in (-2, -1, 1, 2)}
-    mates = [
+    twin = seq_of(half, ring, 1 - core)
+    facing = RING - 1 - ring
+    sharers = [
         None,
-        seq_of(half, ring, 1 - core),
+        seq_of(half, facing, core),
         seq_of(1 - half, ring, core),
-        seq_of(1 - half, ring, 1 - core),
-    ]
+        seq_of(1 - half, facing, core),
+    ]
+    line = (ring // LINE) * LINE
+
+    def on_line(k):
+        return seq_of(half, line + (ring + LINE + k) % LINE, core)
+
     near = {k: (seq + SEQ + k) % SEQ for k in (-3, -2, -1, 1, 2, 3)}
 
     def to_band(k):
@@ -316,7 +323,8 @@
         load.start()
 
     barrier = pltpu.get_barrier_semaphore()
-    others = [{"seq": other} for other in list(near.values()) + list(along.values()) + mates[1:]]
+    others = [{"seq": other} for other in list(near.values()) + sharers[1:] + [twin]]
+    others += [{"seq": on_line(k)} for k in (1, 2, 3)]
     others += [{"band": to_band(k)} for k in range(1, BANDS)]
     for other in others:
         pl.semaphore_signal(barrier, inc=1, device_id=other, device_id_type=MESH)
@@ -355,27 +363,15 @@
     kv[0, 144:272] = qkv[:, 256:384].T.astype(BF16)
     q_all[0] = qkv[:, 0:128].astype(BF16)
 
-    def kv_copy(src, dst, sem, hops, rows=None):
-        where, landed = kv.at[src], kv.at[dst]
-        arrival = dst
-        if rows is not None:
-            where, landed = where.at[pl.ds(*rows)], landed.at[pl.ds(*rows)]
-            arrival = dst if rows[0] == 0 else 0
-        return remote(where, landed, kv_s.at[sem], kv_r.at[arrival], seq=along[hops])
-
-    upper, lower = (0, 144), (144, 128)
-    one = kv_copy(0, 1, 0, 1)
-    seven = kv_copy(0, 7, 1, -1)
-    two = kv_copy(0, 2, 2, 2)
-    six = kv_copy(0, 6, 3, -2)
-    three = kv_copy(1, 3, 4, 2)
-    five = kv_copy(7, 5, 5, -2)
-    four_up = kv_copy(2, 4, 6, 2, upper)
-    four_low = kv_copy(6, 4, 7, -2, lower)
+    def kv_copy(src, dst, sem, other):
+        return remote(kv.at[src], kv.at[dst], kv_s.at[sem], kv_r.at[dst], seq=other)
+
+    kv_direct = [kv_copy(0, j, j, sharers[j]) for j in (1, 2, 3)]
+    kv_twin = [kv_copy(j, 4 + j, 4 + j, twin) for j in range(4)]
     q_copies = [
-        remote(q_all.at[0], q_all.at[k], q_s.at[k], q_r.at[k], seq=mates[k]) for k in (1, 2, 3)
-    ]
-    for copy in [one, seven] + q_copies + [two, six]:
+        remote(q_all.at[0], q_all.at[k], q_s.at[k], q_r.at[k], seq=on_line(k)) for k in (1, 2, 3)
+    ]
+    for copy in kv_direct + q_copies + [kv_twin[0]]:
         copy.start()
 
     across = row * 2 + 1 - side
@@ -404,6 +400,8 @@
     keep = jnp.broadcast_to(map_v[...].astype(F32), (128, 128)).T
     keep = jnp.concatenate([keep, keep], axis=1)
     lr_tok = jnp.dot(floats.astype(BF16), wlr[...], preferred_element_type=F32)
+    kv_direct[1].wait_recv()
+    kv_twin[2].start()
     for copy in q_copies:
         copy.wait_recv()
     queries = jnp.concatenate([q_all[k] for k in range(4)], axis=0)
@@ -436,26 +434,21 @@
         fade = jnp.exp(state[0] - top)
         return top, state[1] * fade + block_sum, state[2] * fade + mixed
 
-    state = attend(None, [0])
-    one.wait_recv()
-    three.start()
-    seven.wait_recv()
-    five.start()
-    state = attend(state, [1, 7])
+    kv_direct[0].wait_recv()
+    kv_twin[1].start()
+    kv_twin[0].wait_recv()
+    state = attend(None, [0, 4])
+    state = attend(state, [1, 2])
+    kv_direct[2].wait_recv()
+    kv_twin[3].start()
     m_arrivals[0].wait_recv()
     for send in m_relay:
         send.start()
-    two.wait_recv()
-    four_up.start()
-    six.wait_recv()
-    four_low.start()
-    state = attend(state, [2, 6])
-    three.wait_recv()
-    five.wait_recv()
-    state = attend(state, [3, 5])
-    four_up.wait_recv()
-    four_low.wait_recv()
-    top, total, mixed = attend(state, [4])
+    kv_twin[1].wait_recv()
+    kv_twin[2].wait_recv()
+    state = attend(state, [5, 6])
+    kv_twin[3].wait_recv()
+    top, total, mixed = attend(state, [3, 7])
 
     mixed = mixed / total
     o_copies = []
@@ -465,9 +458,11 @@
         st_send[k, 0:4] = jnp.broadcast_to(top[:, lanes], (4, 128))
         st_send[k, 4:8] = jnp.broadcast_to(total[:, lanes], (4, 128))
         o_copies.append(
-            remote(st_send.at[k], st_recv.at[k], st_s.at[k], st_r.at[k], seq=mates[k])
-        )
-        o_copies.append(remote(o_send.at[k], o_recv.at[k], o_s.at[k], o_r.at[k], seq=mates[k]))
+            remote(st_send.at[k], st_recv.at[k], st_s.at[k], st_r.at[k], seq=on_line(-k))
+        )
+        o_copies.append(
+            remote(o_send.at[k], o_recv.at[k], o_s.at[k], o_r.at[k], seq=on_line(-k))
+        )
     for copy in o_copies:
         copy.start()
     for copy in o_copies:
@@ -552,7 +547,7 @@
     trunk_ref[...] = (tok_all[band].astype(F32) + summed).astype(BF16)
     for send in tok_sends + q_copies + m_own + m_relay + o_copies + att_sends + edges + wc_sends:
         send.wait_send()
-    for send in [one, two, three, five, six, seven, four_up, four_low]:
+    for send in kv_direct + kv_twin:
         send.wait_send()
 
 

time: 58.2 us -> 55.9 us (0.960)
  Pallas kernels: 55.4 us -> 53.1 us
    pallas_call x1, Pallas kernels: 55.4 us -> 53.1 us  [local(): pl.pallas_call(trunk_kernel, out_shape=(jax.ShapeDtypeStruct((BINS, 128),...]
where the time goes in v4:
time: 55.9 us; the launch traced here: 55.8 us
  Pallas kernels  53.1 us (95%)
  local copies, waits for them, and re-layouts  1.99 us (4%)
  between operations  0.65 us (1%)
    pallas_call x1, Pallas kernels, local(): pl.pallas_call(trunk_kernel, out_shape=(jax.ShapeDtypeStruct((BINS, 128),...  53.1 us
    unnamed x4, local copies, waits for them, and re-layouts  1.99 us

profile of v4, /device:TPU:1, one launch (start us, length us, event | category | flops | bytes accessed | tf_op | source)
XLA Modules:
  0.0 55.8 jit_solution(17187123323053105204)
XLA Ops:
  0.6 53.1 %shard_map.140 = (bf16[128,128]{1,0:T(8,128)(2,1)}, f32[32,128]{1,0:T(8,128)}) custom-call(bf16[128,128]{1,0:T(8,128)(2,1)} %tok_ref.1, s32[1,128]{1,0:T(1,128)} %bitcast.6, f32[1,1024]{1,0:T(1,128)} %bitcast.5, bf16[1024,128]{1,0:T(8,128)(2,1)} %wq_ref.1, bf16[1024,128]{1,0:T(8,128)(2,1)} %wk_ref.1, bf16[1024,128]{1,0:T(8,128)(2,1)} %wv_ref.1, ...), custom_call_target="tpu_custom_call" | custom-call | tf_op jit(solution)/shard_map/pallas_call | solution.py:572
  53.8 0.0 copy-start
  53.8 1.4 %copy.17 = bf16[128,128]{1,0:T(8,128)(2,1)} copy(bf16[128,128]{1,0:T(8,128)(2,1)} %get-tuple-element.8) | data formatting | bytes 65536
  55.2 0.0 copy-done
  55.2 0.6 %copy.18 = f32[128,32]{0,1:T(8,128)} copy(f32[128,32]{0,1:T(8,128)S(1)} %bitcast.4) | data formatting | bytes 32768
Async XLA Ops:
  53.8 1.4 %copy-start = (f32[32,128]{1,0:T(8,128)S(1)}, f32[32,128]{1,0:T(8,128)}, u32[]{:S(2)}) copy-start(f32[32,128]{1,0:T(8,128)} %get-tuple-element.5) | copy-start | bytes 49156

commit v5 on v4

--- a/solution.py
+++ b/solution.py
@@ -35,7 +35,8 @@
 LEAD = 8
 WIDE0 = 44
 WIDE1 = 40
-GROUP = 4
+GROUP = 8
+LATE = 16
 
 
 def norm_gelu(field, half_gain, keep):
@@ -43,7 +44,7 @@
     inv = lax.rsqrt(squares + HEAD * EPS)
     if keep is not None:
         inv = jnp.where(keep, inv, 0.0)
-    half = field * inv * half_gain
+    half = (field * inv * half_gain).astype(BF16)
     inner = half * (1.5957691216057308 + 0.285419265090401 * (half * half))
     return half + half * jnp.tanh(inner)
 
@@ -69,8 +70,11 @@
     loads,
 ):
     length = SEQ * BINS
-    lf[...] = leftbuf[...].astype(F32)
-    rf[0:192] = rightbuf[pl.ds(pl.multiple_of(band * DIAG, DIAG), 192)].astype(F32)
+    bins = lax.broadcasted_iota(jnp.int32, (160, 128), 0) + (seq * BINS - 16)
+    lf[...] = jnp.where((bins >= 0) & (bins < length), leftbuf[...].astype(F32), 0.0)
+    bins = lax.broadcasted_iota(jnp.int32, (192, 128), 0) + (seq * BINS + band * DIAG - 16)
+    window = rightbuf[pl.ds(pl.multiple_of(band * DIAG, DIAG), 192)].astype(F32)
+    rf[0:192] = jnp.where((bins >= 0) & (bins < length), window, 0.0)
     for a in range(CHUNK):
         lp[a] = lf[pl.ds(LEAD + a, LANES, stride=CHUNK)]
     for t in range(WIDE0 + CHUNK - 1):
@@ -100,15 +104,16 @@
     weight = weight_ref[...].reshape(1, 1, 128)
 
     def put(dst, where, act, reach):
-        dst[where, pl.ds(reach, CHUNK)] = act.astype(BF16)
-        before = pltpu.roll(act[CHUNK - reach :], 1, 1)
-        after = pltpu.roll(act[:reach], LANES - 1, 1)
+        dst[where, pl.ds(reach, CHUNK)] = act
+        before = pltpu.roll(act[CHUNK - reach :].astype(F32), 1, 1)
+        after = pltpu.roll(act[:reach].astype(F32), LANES - 1, 1)
         dst[where, pl.ds(0, reach)] = before.astype(BF16)
         dst[where, pl.ds(reach + CHUNK, reach)] = after.astype(BF16)
 
     def first_act(delta):
-        keep = inside(band * DIAG + delta - 6)
-        put(act0, delta, norm_gelu(start_field(delta), gain0, keep), 1)
+        diag = band * DIAG + delta - 6
+        known = jnp.where((diag >= 0) & (diag < BANDS * DIAG), 1.0, 0.0)
+        put(act0, delta, norm_gelu(start_field(delta), gain0 * known, None), 1)
 
     def conv(src, layer, slabs, reach):
         taps = jnp.concatenate(
@@ -139,29 +144,27 @@
             keep = inside(band * DIAG + diag + g - 4)
             put(act1, diag + g, norm_gelu(value, gain1, keep), 2)
 
-    @pl.loop(0, 2)
-    def _(step):
-        for g in range(GROUP):
-            first_act(step * GROUP + g)
+    for g in range(GROUP + 4):
+        first_act(g)
 
     for load in loads:
         load.wait()
 
     def conv0(step):
         slab = step * GROUP + 2
-        return conv(act0, 0, [slab, slab + 2], 1)
+        return conv(act0, 0, [slab + g for g in range(0, GROUP, 2)], 1)
 
     def grow(step, term):
         fresh = conv0(step)
         second_act(step - 1, term)
         for g in range(GROUP):
-            first_act(step * GROUP + 8 + g)
+            first_act(step * GROUP + GROUP + 4 + g)
         return fresh
 
     steps = WIDE1 // GROUP
     term = conv0(0)
     for g in range(GROUP):
-        first_act(8 + g)
+        first_act(GROUP + 4 + g)
     term = lax.fori_loop(1, steps - 1, grow, term)
     fresh = conv0(steps - 1)
     second_act(steps - 2, term)
@@ -170,13 +173,13 @@
     lane = lax.broadcasted_iota(jnp.int32, shape, 2)
 
     def conv1(step):
-        slab = step * GROUP + 4
-        return conv(act1, 1, [slab, slab + 1], 2)
+        slab = step * LATE + 4
+        return conv(act1, 1, [slab + g for g in range(LATE) if g % 4 < 2], 2)
 
     def finish(step, term, found):
-        diag = step * GROUP
-        for g in range(GROUP):
-            pair, half = g % 2, g // 2
+        diag = step * LATE
+        for g in range(LATE):
+            pair, half = (g // 4) * 2 + g % 2, g % 4 // 2
             block = term[pair * ROWS : (pair + 1) * ROWS, half * 128 : (half + 1) * 128]
             value = block.reshape(shape) + field1[diag + g + 4].astype(F32) + bias1
             contact = jnp.sum(value * weight, axis=-1, keepdims=True)
@@ -188,7 +191,7 @@
         fresh = conv1(step)
         return fresh, finish(step - 1, term, found)
 
-    steps = DIAG // GROUP
+    steps = DIAG // LATE
     term, found = lax.fori_loop(1, steps, last, (conv1(0), jnp.zeros(shape, F32)))
     found = finish(steps - 1, term, found)
     found = jnp.where(spot + band * DIAG + lane < length, found, 0.0)
@@ -395,8 +398,6 @@
         + [(row_peer(-k, side), k) for k in (1, 2, 3)]
         + [(row_peer(-k, 1 - side), 3 + k) for k in (1, 2, 3)]
     ]
-    for send in m_own:
-        send.start()
     keep = jnp.broadcast_to(map_v[...].astype(F32), (128, 128)).T
     keep = jnp.concatenate([keep, keep], axis=1)
     lr_tok = jnp.dot(floats.astype(BF16), wlr[...], preferred_element_type=F32)
@@ -441,8 +442,7 @@
     state = attend(state, [1, 2])
     kv_direct[2].wait_recv()
     kv_twin[3].start()
-    m_arrivals[0].wait_recv()
-    for send in m_relay:
+    for send in m_own:
         send.start()
     kv_twin[1].wait_recv()
     kv_twin[2].wait_recv()
@@ -465,6 +465,9 @@
         )
     for copy in o_copies:
         copy.start()
+    m_arrivals[0].wait_recv()
+    for send in m_relay:
+        send.start()
     for copy in o_copies:
         copy.wait_recv()
     tops = [top[:, 0:128]] + [st_recv[k, 0:1] for k in (1, 2, 3)]
@@ -513,11 +516,11 @@
         )
         for k in range(1, BANDS)
     ]
-    for send in wc_sends:
-        send.start()
     wcol_all[band] = wout[:, pl.ds(pl.multiple_of(band * 128, 128), 128)]
     for copy in edges:
         copy.wait_recv()
+    for send in wc_sends:
+        send.start()
     pair_map(
         seq,
         band,

time: 55.9 us -> 53.7 us (0.961)
  Pallas kernels: 53.1 us -> 50.9 us
    pallas_call x1, Pallas kernels: 53.1 us -> 50.9 us  [local(): pl.pallas_call(trunk_kernel, out_shape=(jax.ShapeDtypeStruct((BINS, 128),...]
where the time goes in v5:
time: 53.7 us; the launch traced here: 53.6 us
  Pallas kernels  50.9 us (95%)
  local copies, waits for them, and re-layouts  1.99 us (4%)
  between operations  0.65 us (1%)
    pallas_call x1, Pallas kernels, local(): pl.pallas_call(trunk_kernel, out_shape=(jax.ShapeDtypeStruct((BINS, 128),...  50.9 us
    unnamed x4, local copies, waits for them, and re-layouts  1.99 us

profile of v5, /device:TPU:1, one launch (start us, length us, event | category | flops | bytes accessed | tf_op | source)
XLA Modules:
  0.0 53.6 jit_solution(7758427699337768087)
XLA Ops:
  0.6 50.9 %shard_map.140 = (bf16[128,128]{1,0:T(8,128)(2,1)}, f32[32,128]{1,0:T(8,128)}) custom-call(bf16[128,128]{1,0:T(8,128)(2,1)} %tok_ref.1, s32[1,128]{1,0:T(1,128)} %bitcast.6, f32[1,1024]{1,0:T(1,128)} %bitcast.5, bf16[1024,128]{1,0:T(8,128)(2,1)} %wq_ref.1, bf16[1024,128]{1,0:T(8,128)(2,1)} %wk_ref.1, bf16[1024,128]{1,0:T(8,128)(2,1)} %wv_ref.1, ...), custom_call_target="tpu_custom_call" | custom-call | tf_op jit(solution)/shard_map/pallas_call | solution.py:575
  51.6 0.0 copy-start
  51.6 1.4 %copy.17 = bf16[128,128]{1,0:T(8,128)(2,1)} copy(bf16[128,128]{1,0:T(8,128)(2,1)} %get-tuple-element.8) | data formatting | bytes 65536
  53.0 0.0 copy-done
  53.0 0.6 %copy.18 = f32[128,32]{0,1:T(8,128)} copy(f32[128,32]{0,1:T(8,128)S(1)} %bitcast.4) | data formatting | bytes 32768
Async XLA Ops:
  51.6 1.4 %copy-start = (f32[32,128]{1,0:T(8,128)S(1)}, f32[32,128]{1,0:T(8,128)}, u32[]{:S(2)}) copy-start(f32[32,128]{1,0:T(8,128)} %get-tuple-element.5) | copy-start | bytes 49156

commit v6 on v5

--- a/solution.py
+++ b/solution.py
@@ -278,17 +278,19 @@
         return half_ * (2 * RING) + ring_ * 2 + core_
 
     twin = seq_of(half, ring, 1 - core)
-    facing = RING - 1 - ring
+    facing = ring + 1 - 2 * (ring % 2)
     sharers = [
         None,
         seq_of(half, facing, core),
         seq_of(1 - half, ring, core),
         seq_of(1 - half, facing, core),
     ]
-    line = (ring // LINE) * LINE
+    pair = ring // 2
+    turn = ring + pair // 2
 
     def on_line(k):
-        return seq_of(half, line + (ring + LINE + k) % LINE, core)
+        other = (pair + LINE + k) % LINE
+        return seq_of(half, 2 * other + (turn + other // 2) % 2, core)
 
     near = {k: (seq + SEQ + k) % SEQ for k in (-3, -2, -1, 1, 2, 3)}
 
@@ -374,7 +376,7 @@
     q_copies = [
         remote(q_all.at[0], q_all.at[k], q_s.at[k], q_r.at[k], seq=on_line(k)) for k in (1, 2, 3)
     ]
-    for copy in kv_direct + q_copies + [kv_twin[0]]:
+    for copy in [kv_direct[2], kv_direct[0], kv_direct[1]] + q_copies + [kv_twin[0]]:
         copy.start()
 
     across = row * 2 + 1 - side
@@ -398,13 +400,23 @@
         + [(row_peer(-k, side), k) for k in (1, 2, 3)]
         + [(row_peer(-k, 1 - side), 3 + k) for k in (1, 2, 3)]
     ]
+    wc_sends = [
+        band_send(
+            wout.at[:, pl.ds(pl.multiple_of(to_band(k) * 128, 128), 128)], wcol_all, wc_s, wc_r, k
+        )
+        for k in range(1, BANDS)
+    ]
+    wcol_all[band] = wout[:, pl.ds(pl.multiple_of(band * 128, 128), 128)]
     keep = jnp.broadcast_to(map_v[...].astype(F32), (128, 128)).T
     keep = jnp.concatenate([keep, keep], axis=1)
     lr_tok = jnp.dot(floats.astype(BF16), wlr[...], preferred_element_type=F32)
-    kv_direct[1].wait_recv()
-    kv_twin[2].start()
+    for j in (2, 1, 3):
+        kv_direct[j - 1].wait_recv()
+        kv_twin[j].start()
     for copy in q_copies:
         copy.wait_recv()
+    for send in m_own + wc_sends:
+        send.start()
     queries = jnp.concatenate([q_all[k] for k in range(4)], axis=0)
 
     def attend(state, slots):
@@ -435,15 +447,9 @@
         fade = jnp.exp(state[0] - top)
         return top, state[1] * fade + block_sum, state[2] * fade + mixed
 
-    kv_direct[0].wait_recv()
-    kv_twin[1].start()
     kv_twin[0].wait_recv()
     state = attend(None, [0, 4])
     state = attend(state, [1, 2])
-    kv_direct[2].wait_recv()
-    kv_twin[3].start()
-    for send in m_own:
-        send.start()
     kv_twin[1].wait_recv()
     kv_twin[2].wait_recv()
     state = attend(state, [5, 6])
@@ -510,17 +516,20 @@
     ]
     for copy in edges:
         copy.start()
-    wc_sends = [
-        band_send(
-            wout.at[:, pl.ds(pl.multiple_of(to_band(k) * 128, 128), 128)], wcol_all, wc_s, wc_r, k
-        )
-        for k in range(1, BANDS)
-    ]
-    wcol_all[band] = wout[:, pl.ds(pl.multiple_of(band * 128, 128), 128)]
+    for k in range(1, BANDS):
+        band_recv(wcol_all, wc_s, wc_r, k).wait_recv()
+    summed = jnp.dot(
+        heads, wcol_all[...].reshape(BANDS * 128, 128), preferred_element_type=F32
+    )
+    trunk_ref[...] = (tok_all[band].astype(F32) + summed).astype(BF16)
+    for send in tok_sends + q_copies + kv_direct + kv_twin + m_own + m_relay + wc_sends:
+        send.wait_send()
+    for send in o_copies + att_sends:
+        send.wait_send()
     for copy in edges:
         copy.wait_recv()
-    for send in wc_sends:
-        send.start()
+    for send in edges:
+        send.wait_send()
     pair_map(
         seq,
         band,
@@ -541,17 +550,6 @@
         plain,
         tap_loads,
     )
-    for k in range(1, BANDS):
-        band_recv(wcol_all, wc_s, wc_r, k).wait_recv()
-    heads = jnp.concatenate([att_all[c] for c in range(BANDS)], axis=1)
-    summed = jnp.dot(
-        heads, wcol_all[...].reshape(BANDS * 128, 128), preferred_element_type=F32
-    )
-    trunk_ref[...] = (tok_all[band].astype(F32) + summed).astype(BF16)
-    for send in tok_sends + q_copies + m_own + m_relay + o_copies + att_sends + edges + wc_sends:
-        send.wait_send()
-    for send in kv_direct + kv_twin:
-        send.wait_send()
 
 
 def local(

time: 53.7 us -> 54.3 us (1.011)
  Pallas kernels: 50.9 us -> 51.5 us
    pallas_call x1, Pallas kernels: 50.9 us -> 51.5 us  [local(): pl.pallas_call(trunk_kernel, out_shape=(jax.ShapeDtypeStruct((BINS, 128),...]
where the time goes in v6:
time: 54.3 us; the launch traced here: 54.2 us
  Pallas kernels  51.5 us (95%)
  local copies, waits for them, and re-layouts  1.99 us (4%)
  between operations  0.65 us (1%)
    pallas_call x1, Pallas kernels, local(): pl.pallas_call(trunk_kernel, out_shape=(jax.ShapeDtypeStruct((BINS, 128),...  51.5 us
    unnamed x4, local copies, waits for them, and re-layouts  1.99 us

profile of v6, /device:TPU:1, one launch (start us, length us, event | category | flops | bytes accessed | tf_op | source)
XLA Modules:
  0.0 54.2 jit_solution(8811462727095991118)
XLA Ops:
  0.6 51.5 %shard_map.140 = (bf16[128,128]{1,0:T(8,128)(2,1)}, f32[32,128]{1,0:T(8,128)}) custom-call(bf16[128,128]{1,0:T(8,128)(2,1)} %tok_ref.1, s32[1,128]{1,0:T(1,128)} %bitcast.6, f32[1,1024]{1,0:T(1,128)} %bitcast.5, bf16[1024,128]{1,0:T(8,128)(2,1)} %wq_ref.1, bf16[1024,128]{1,0:T(8,128)(2,1)} %wk_ref.1, bf16[1024,128]{1,0:T(8,128)(2,1)} %wv_ref.1, ...), custom_call_target="tpu_custom_call" | custom-call | tf_op jit(solution)/shard_map/pallas_call | solution.py:573
  52.2 0.0 copy-start
  52.2 1.4 %copy.17 = bf16[128,128]{1,0:T(8,128)(2,1)} copy(bf16[128,128]{1,0:T(8,128)(2,1)} %get-tuple-element.8) | data formatting | bytes 65536
  53.6 0.0 copy-done
  53.6 0.6 %copy.18 = f32[128,32]{0,1:T(8,128)} copy(f32[128,32]{0,1:T(8,128)S(1)} %bitcast.4) | data formatting | bytes 32768
Async XLA Ops:
  52.2 1.4 %copy-start = (f32[32,128]{1,0:T(8,128)S(1)}, f32[32,128]{1,0:T(8,128)}, u32[]{:S(2)}) copy-start(f32[32,128]{1,0:T(8,128)} %get-tuple-element.5) | copy-start | bytes 49156

commit v7 on v6

--- a/solution.py
+++ b/solution.py
@@ -294,11 +294,13 @@
 
     near = {k: (seq + SEQ + k) % SEQ for k in (-3, -2, -1, 1, 2, 3)}
 
+    hops = [None, (2, 1), (1, 1), (3, 1), (0, 1), (2, 0), (1, 0), (3, 0)]
+
     def to_band(k):
-        return (band + k) % BANDS
+        return (row + hops[k][0]) % 4 * 2 + (side + hops[k][1]) % 2
 
     def from_band(k):
-        return (band + BANDS - k) % BANDS
+        return (row + 4 - hops[k][0]) % 4 * 2 + (side + hops[k][1]) % 2
 
     loads = [
         pltpu.make_async_copy(tok_ref, tok_all.at[band], local_sem.at[0]),
@@ -376,7 +378,9 @@
     q_copies = [
         remote(q_all.at[0], q_all.at[k], q_s.at[k], q_r.at[k], seq=on_line(k)) for k in (1, 2, 3)
     ]
-    for copy in [kv_direct[2], kv_direct[0], kv_direct[1]] + q_copies + [kv_twin[0]]:
+    for copy in [kv_direct[2], q_copies[1], kv_direct[0], kv_direct[1]]:
+        copy.start()
+    for copy in [q_copies[0], q_copies[2], kv_twin[0]]:
         copy.start()
 
     across = row * 2 + 1 - side
@@ -448,17 +452,14 @@
         return top, state[1] * fade + block_sum, state[2] * fade + mixed
 
     kv_twin[0].wait_recv()
-    state = attend(None, [0, 4])
-    state = attend(state, [1, 2])
-    kv_twin[1].wait_recv()
-    kv_twin[2].wait_recv()
-    state = attend(state, [5, 6])
-    kv_twin[3].wait_recv()
-    top, total, mixed = attend(state, [3, 7])
+    state = attend(None, [0, 4, 1, 2])
+    for copy in kv_twin[1:]:
+        copy.wait_recv()
+    top, total, mixed = attend(state, [3, 5, 6, 7])
 
     mixed = mixed / total
     o_copies = []
-    for k in (1, 2, 3):
+    for k in (2, 1, 3):
         lanes = slice(k * 128, (k + 1) * 128)
         o_send[k] = mixed[:, lanes].astype(BF16)
         st_send[k, 0:4] = jnp.broadcast_to(top[:, lanes], (4, 128))
@@ -507,9 +508,9 @@
 
     own = rightbuf.at[pl.ds(16, 128)]
     edges = [
+        edge(rightbuf.at[pl.ds(16, 16)], rightbuf.at[pl.ds(400, 16)], 2, near[-3]),
         edge(own, rightbuf.at[pl.ds(272, 128)], 1, near[-2]),
         edge(own, rightbuf.at[pl.ds(144, 128)], 0, near[-1]),
-        edge(rightbuf.at[pl.ds(16, 16)], rightbuf.at[pl.ds(400, 16)], 2, near[-3]),
         edge(rightbuf.at[pl.ds(128, 16)], rightbuf.at[pl.ds(0, 16)], 3, near[1]),
         edge(leftbuf.at[pl.ds(16, 16)], leftbuf.at[pl.ds(144, 16)], 4, near[-1]),
         edge(leftbuf.at[pl.ds(128, 16)], leftbuf.at[pl.ds(0, 16)], 5, near[1]),

time: 54.3 us -> 52.7 us (0.971)
  Pallas kernels: 51.5 us -> 50 us
    pallas_call x1, Pallas kernels: 51.5 us -> 50 us  [local(): pl.pallas_call(trunk_kernel, out_shape=(jax.ShapeDtypeStruct((BINS, 128),...]
where the time goes in v7:
time: 52.7 us; the launch traced here: 52.6 us
  Pallas kernels  50 us (95%)
  local copies, waits for them, and re-layouts  1.99 us (4%)
  between operations  0.65 us (1%)
    pallas_call x1, Pallas kernels, local(): pl.pallas_call(trunk_kernel, out_shape=(jax.ShapeDtypeStruct((BINS, 128),...  50 us
    unnamed x4, local copies, waits for them, and re-layouts  1.99 us

profile of v7, /device:TPU:1, one launch (start us, length us, event | category | flops | bytes accessed | tf_op | source)
XLA Modules:
  0.0 52.6 jit_solution(4697226162527824451)
XLA Ops:
  0.6 50.0 %shard_map.140 = (bf16[128,128]{1,0:T(8,128)(2,1)}, f32[32,128]{1,0:T(8,128)}) custom-call(bf16[128,128]{1,0:T(8,128)(2,1)} %tok_ref.1, s32[1,128]{1,0:T(1,128)} %bitcast.6, f32[1,1024]{1,0:T(1,128)} %bitcast.5, bf16[1024,128]{1,0:T(8,128)(2,1)} %wq_ref.1, bf16[1024,128]{1,0:T(8,128)(2,1)} %wk_ref.1, bf16[1024,128]{1,0:T(8,128)(2,1)} %wv_ref.1, ...), custom_call_target="tpu_custom_call" | custom-call | tf_op jit(solution)/shard_map/pallas_call | solution.py:574
  50.6 0.0 copy-start
  50.6 1.4 %copy.17 = bf16[128,128]{1,0:T(8,128)(2,1)} copy(bf16[128,128]{1,0:T(8,128)(2,1)} %get-tuple-element.8) | data formatting | bytes 65536
  52.0 0.0 copy-done
  52.0 0.6 %copy.18 = f32[128,32]{0,1:T(8,128)} copy(f32[128,32]{0,1:T(8,128)S(1)} %bitcast.4) | data formatting | bytes 32768
Async XLA Ops:
  50.6 1.4 %copy-start = (f32[32,128]{1,0:T(8,128)S(1)}, f32[32,128]{1,0:T(8,128)}, u32[]{:S(2)}) copy-start(f32[32,128]{1,0:T(8,128)} %get-tuple-element.5) | copy-start | bytes 49156

commit v8 on v7

--- a/solution.py
+++ b/solution.py
@@ -326,16 +326,14 @@
         for p in range(3)
         for second in range(2)
     ]
-    for load in loads:
-        load.start()
-
     barrier = pltpu.get_barrier_semaphore()
-    others = [{"seq": other} for other in list(near.values()) + sharers[1:] + [twin]]
-    others += [{"seq": on_line(k)} for k in (1, 2, 3)]
-    others += [{"band": to_band(k)} for k in range(1, BANDS)]
+    others = [{"band": to_band(k)} for k in range(1, BANDS)]
+    others += [{"seq": on_line(k)} for k in (2, 1, 3)]
+    others += [{"seq": near[k]} for k in (-3, 3, -2, 2, -1, 1)]
+    others += [{"seq": other} for other in sharers[1:] + [twin]]
     for other in others:
         pl.semaphore_signal(barrier, inc=1, device_id=other, device_id_type=MESH)
-    for load in tap_loads:
+    for load in loads + tap_loads:
         load.start()
     for layer in range(2):
         for p in range(3):

time: 52.7 us -> 52.4 us (level)
  no operation moved by 1% of the time
where the time goes in v8:
time: 52.4 us; the launch traced here: 52.3 us
  Pallas kernels  49.6 us (95%)
  local copies, waits for them, and re-layouts  1.99 us (4%)
  between operations  0.65 us (1%)
    pallas_call x1, Pallas kernels, local(): pl.pallas_call(trunk_kernel, out_shape=(jax.ShapeDtypeStruct((BINS, 128),...  49.6 us
    unnamed x4, local copies, waits for them, and re-layouts  1.99 us

profile of v8, /device:TPU:1, one launch (start us, length us, event | category | flops | bytes accessed | tf_op | source)
XLA Modules:
  0.0 52.3 jit_solution(2118233884236801019)
XLA Ops:
  0.6 49.6 %shard_map.140 = (bf16[128,128]{1,0:T(8,128)(2,1)}, f32[32,128]{1,0:T(8,128)}) custom-call(bf16[128,128]{1,0:T(8,128)(2,1)} %tok_ref.1, s32[1,128]{1,0:T(1,128)} %bitcast.6, f32[1,1024]{1,0:T(1,128)} %bitcast.5, bf16[1024,128]{1,0:T(8,128)(2,1)} %wq_ref.1, bf16[1024,128]{1,0:T(8,128)(2,1)} %wk_ref.1, bf16[1024,128]{1,0:T(8,128)(2,1)} %wv_ref.1, ...), custom_call_target="tpu_custom_call" | custom-call | tf_op jit(solution)/shard_map/pallas_call | solution.py:572
  50.3 0.0 copy-start
  50.3 1.4 %copy.17 = bf16[128,128]{1,0:T(8,128)(2,1)} copy(bf16[128,128]{1,0:T(8,128)(2,1)} %get-tuple-element.8) | data formatting | bytes 65536
  51.7 0.0 copy-done
  51.7 0.6 %copy.18 = f32[128,32]{0,1:T(8,128)} copy(f32[128,32]{0,1:T(8,128)S(1)} %bitcast.4) | data formatting | bytes 32768
Async XLA Ops:
  50.3 1.4 %copy-start = (f32[32,128]{1,0:T(8,128)S(1)}, f32[32,128]{1,0:T(8,128)}, u32[]{:S(2)}) copy-start(f32[32,128]{1,0:T(8,128)} %get-tuple-element.5) | copy-start | bytes 49156

commit v9 on v8

--- a/solution.py
+++ b/solution.py
@@ -412,13 +412,15 @@
     keep = jnp.broadcast_to(map_v[...].astype(F32), (128, 128)).T
     keep = jnp.concatenate([keep, keep], axis=1)
     lr_tok = jnp.dot(floats.astype(BF16), wlr[...], preferred_element_type=F32)
-    for j in (2, 1, 3):
+    kv_direct[1].wait_recv()
+    kv_twin[2].start()
+    for send in wc_sends:
+        send.start()
+    for j in (1, 3):
         kv_direct[j - 1].wait_recv()
         kv_twin[j].start()
     for copy in q_copies:
         copy.wait_recv()
-    for send in m_own + wc_sends:
-        send.start()
     queries = jnp.concatenate([q_all[k] for k in range(4)], axis=0)
 
     def attend(state, slots):
@@ -470,6 +472,8 @@
         )
     for copy in o_copies:
         copy.start()
+    for send in m_own:
+        send.start()
     m_arrivals[0].wait_recv()
     for send in m_relay:
         send.start()

time: 52.4 us -> 52.2 us (level)
  no operation moved by 1% of the time
where the time goes in v9:
time: 52.2 us; the launch traced here: 52 us
  Pallas kernels  49.3 us (94%)
  local copies, waits for them, and re-layouts  1.99 us (4%)
  between operations  0.65 us (1%)
    pallas_call x1, Pallas kernels, local(): pl.pallas_call(trunk_kernel, out_shape=(jax.ShapeDtypeStruct((BINS, 128),...  49.3 us
    unnamed x4, local copies, waits for them, and re-layouts  1.99 us

profile of v9, /device:TPU:1, one launch (start us, length us, event | category | flops | bytes accessed | tf_op | source)
XLA Modules:
  0.0 52.0 jit_solution(13453875012256810587)
XLA Ops:
  0.6 49.3 %shard_map.140 = (bf16[128,128]{1,0:T(8,128)(2,1)}, f32[32,128]{1,0:T(8,128)}) custom-call(bf16[128,128]{1,0:T(8,128)(2,1)} %tok_ref.1, s32[1,128]{1,0:T(1,128)} %bitcast.6, f32[1,1024]{1,0:T(1,128)} %bitcast.5, bf16[1024,128]{1,0:T(8,128)(2,1)} %wq_ref.1, bf16[1024,128]{1,0:T(8,128)(2,1)} %wk_ref.1, bf16[1024,128]{1,0:T(8,128)(2,1)} %wv_ref.1, ...), custom_call_target="tpu_custom_call" | custom-call | tf_op jit(solution)/shard_map/pallas_call | solution.py:576
  50.0 0.0 copy-start
  50.0 1.4 %copy.17 = bf16[128,128]{1,0:T(8,128)(2,1)} copy(bf16[128,128]{1,0:T(8,128)(2,1)} %get-tuple-element.8) | data formatting | bytes 65536
  51.4 0.0 copy-done
  51.4 0.6 %copy.18 = f32[128,32]{0,1:T(8,128)} copy(f32[128,32]{0,1:T(8,128)S(1)} %bitcast.4) | data formatting | bytes 32768
Async XLA Ops:
  50.0 1.4 %copy-start = (f32[32,128]{1,0:T(8,128)S(1)}, f32[32,128]{1,0:T(8,128)}, u32[]{:S(2)}) copy-start(f32[32,128]{1,0:T(8,128)} %get-tuple-element.5) | copy-start | bytes 49156

commit v10 on v9

--- a/solution.py
+++ b/solution.py
@@ -67,7 +67,6 @@
     act1,
     taps_w,
     plain,
-    loads,
 ):
     length = SEQ * BINS
     bins = lax.broadcasted_iota(jnp.int32, (160, 128), 0) + (seq * BINS - 16)
@@ -146,9 +145,6 @@
 
     for g in range(GROUP + 4):
         first_act(g)
-
-    for load in loads:
-        load.wait()
 
     def conv0(step):
         slab = step * GROUP + 2
@@ -492,15 +488,23 @@
     att_sends = [band_send(att_all.at[band], att_all, att_s, att_r, k) for k in range(1, BANDS)]
     for send in att_sends:
         send.start()
-    for copy in m_arrivals[1:]:
+
+    def fold(total, side_):
+        slots = [row_peer(k, side_) for k in range(4)]
+        heads_ = jnp.concatenate([att_all[slot] for slot in slots], axis=1)
+        folded = jnp.concatenate([m_all[slot] for slot in slots], axis=0)
+        return total + jnp.dot(heads_, folded, preferred_element_type=F32)
+
+    for copy in m_arrivals[1:4]:
         copy.wait_recv()
-    for k in range(1, BANDS):
+    for k in (5, 6, 7):
         band_recv(att_all, att_s, att_r, k).wait_recv()
-
-    heads = jnp.concatenate([att_all[c] for c in range(BANDS)], axis=1)
-    both = lr_tok + jnp.dot(
-        heads, m_all[...].reshape(BANDS * 128, 256), preferred_element_type=F32
-    )
+    both = fold(lr_tok, side)
+    for copy in m_arrivals[4:]:
+        copy.wait_recv()
+    for k in (1, 2, 3, 4):
+        band_recv(att_all, att_s, att_r, k).wait_recv()
+    both = fold(both, 1 - side)
     both = (both * keep).astype(BF16)
     leftbuf[16:144] = both[:, 0:128]
     rightbuf[16:144] = both[:, 128:256]
@@ -521,6 +525,7 @@
         copy.start()
     for k in range(1, BANDS):
         band_recv(wcol_all, wc_s, wc_r, k).wait_recv()
+    heads = jnp.concatenate([att_all[c] for c in range(BANDS)], axis=1)
     summed = jnp.dot(
         heads, wcol_all[...].reshape(BANDS * 128, 128), preferred_element_type=F32
     )
@@ -529,6 +534,8 @@
         send.wait_send()
     for send in o_copies + att_sends:
         send.wait_send()
+    for load in tap_loads:
+        load.wait()
     for copy in edges:
         copy.wait_recv()
     for send in edges:
@@ -551,7 +558,6 @@
         act1,
         taps_w,
         plain,
-        tap_loads,
     )
 
 

time: 52.2 us -> 51.9 us (level)
  no operation moved by 1% of the time
where the time goes in v10:
time: 51.9 us; the launch traced here: 51.7 us
  Pallas kernels  49.1 us (95%)
  local copies, waits for them, and re-layouts  1.99 us (4%)
  between operations  0.65 us (1%)
    pallas_call x1, Pallas kernels, local(): pl.pallas_call(trunk_kernel, out_shape=(jax.ShapeDtypeStruct((BINS, 128),...  49.1 us
    unnamed x4, local copies, waits for them, and re-layouts  1.99 us

profile of v10, /device:TPU:1, one launch (start us, length us, event | category | flops | bytes accessed | tf_op | source)
XLA Modules:
  0.0 51.7 jit_solution(2192729622739709910)
XLA Ops:
  0.6 49.1 %shard_map.140 = (bf16[128,128]{1,0:T(8,128)(2,1)}, f32[32,128]{1,0:T(8,128)}) custom-call(bf16[128,128]{1,0:T(8,128)(2,1)} %tok_ref.1, s32[1,128]{1,0:T(1,128)} %bitcast.6, f32[1,1024]{1,0:T(1,128)} %bitcast.5, bf16[1024,128]{1,0:T(8,128)(2,1)} %wq_ref.1, bf16[1024,128]{1,0:T(8,128)(2,1)} %wk_ref.1, bf16[1024,128]{1,0:T(8,128)(2,1)} %wv_ref.1, ...), custom_call_target="tpu_custom_call" | custom-call | tf_op jit(solution)/shard_map/pallas_call | solution.py:582
  49.7 0.0 copy-start
  49.8 1.4 %copy.17 = bf16[128,128]{1,0:T(8,128)(2,1)} copy(bf16[128,128]{1,0:T(8,128)(2,1)} %get-tuple-element.8) | data formatting | bytes 65536
  51.1 0.0 copy-done
  51.1 0.6 %copy.18 = f32[128,32]{0,1:T(8,128)} copy(f32[128,32]{0,1:T(8,128)S(1)} %bitcast.4) | data formatting | bytes 32768
Async XLA Ops:
  49.7 1.4 %copy-start = (f32[32,128]{1,0:T(8,128)S(1)}, f32[32,128]{1,0:T(8,128)}, u32[]{:S(2)}) copy-start(f32[32,128]{1,0:T(8,128)} %get-tuple-element.5) | copy-start | bytes 49156

commit v11 on v10

--- a/solution.py
+++ b/solution.py
@@ -329,8 +329,6 @@
     others += [{"seq": other} for other in sharers[1:] + [twin]]
     for other in others:
         pl.semaphore_signal(barrier, inc=1, device_id=other, device_id_type=MESH)
-    for load in loads + tap_loads:
-        load.start()
     for layer in range(2):
         for p in range(3):
             taps_w[layer, 4 * p + 3, :, 0:128] = jnp.zeros((128, 128), BF16)
@@ -347,6 +345,8 @@
     tok_sends = [band_send(tok_ref, tok_all, tok_s, tok_r, k) for k in range(1, BANDS)]
     for send in tok_sends:
         send.start()
+    for load in loads + tap_loads:
+        load.start()
 
     for load in loads:
         load.wait()

time: 51.9 us -> 51.9 us (level)
  no operation moved by 1% of the time
where the time goes in v11:
time: 51.9 us; the launch traced here: 51.7 us
  Pallas kernels  49.1 us (95%)
  local copies, waits for them, and re-layouts  1.99 us (4%)
  between operations  0.65 us (1%)
    pallas_call x1, Pallas kernels, local(): pl.pallas_call(trunk_kernel, out_shape=(jax.ShapeDtypeStruct((BINS, 128),...  49.1 us
    unnamed x4, local copies, waits for them, and re-layouts  1.99 us

profile of v11, /device:TPU:1, one launch (start us, length us, event | category | flops | bytes accessed | tf_op | source)
XLA Modules:
  0.0 51.7 jit_solution(2168672863651266581)
XLA Ops:
  0.6 49.1 %shard_map.140 = (bf16[128,128]{1,0:T(8,128)(2,1)}, f32[32,128]{1,0:T(8,128)}) custom-call(bf16[128,128]{1,0:T(8,128)(2,1)} %tok_ref.1, s32[1,128]{1,0:T(1,128)} %bitcast.6, f32[1,1024]{1,0:T(1,128)} %bitcast.5, bf16[1024,128]{1,0:T(8,128)(2,1)} %wq_ref.1, bf16[1024,128]{1,0:T(8,128)(2,1)} %wk_ref.1, bf16[1024,128]{1,0:T(8,128)(2,1)} %wv_ref.1, ...), custom_call_target="tpu_custom_call" | custom-call | tf_op jit(solution)/shard_map/pallas_call | solution.py:582
  49.7 0.0 copy-start
  49.8 1.4 %copy.17 = bf16[128,128]{1,0:T(8,128)(2,1)} copy(bf16[128,128]{1,0:T(8,128)(2,1)} %get-tuple-element.8) | data formatting | bytes 65536
  51.1 0.0 copy-done
  51.1 0.6 %copy.18 = f32[128,32]{0,1:T(8,128)} copy(f32[128,32]{0,1:T(8,128)S(1)} %bitcast.4) | data formatting | bytes 32768
Async XLA Ops:
  49.7 1.4 %copy-start = (f32[32,128]{1,0:T(8,128)S(1)}, f32[32,128]{1,0:T(8,128)}, u32[]{:S(2)}) copy-start(f32[32,128]{1,0:T(8,128)} %get-tuple-element.5) | copy-start | bytes 49156
